TPU v7x, 32 devices: a whole 2x2x4 slice. The times are simulated.
32 devices in a mesh: dp: 4 (over y, x), tensor: 8 (over z, core).
Axes of the slice: x: 2, y: 2, z: 4, core: 2. Of those that a mesh axis runs over, the one named last changes fastest.
Arguments:
- image: bfloat16 [8192, 2048], P(('dp', 'tensor')), may hold values from -6 to 6
- text: bfloat16 [4096, 4096], P('dp'), may hold values from -6 to 6
- cotangent: bfloat16 [8192, 2048], P(('dp', 'tensor')), may hold values from -6 to 6
- norm_gains: float32 [3, 2048], replicated, may hold values from 0.5 to 1.5
- norm_shifts: float32 [3, 2048], replicated, may hold values from -1.75 to 1.75
- w_self: bfloat16 [3, 2048, 2048], P(None, None, 'tensor'), may hold values from -1 to 1
- w_self_out: bfloat16 [2048, 2048], P('tensor'), may hold values from -0.5 to 0.5
- w_cross_q: bfloat16 [2048, 2048], P(None, 'tensor'), may hold values from -1 to 1
- w_cross_kv: bfloat16 [2, 2048, 2048], P(None, None, 'tensor'), may hold values from -0.125 to 0.125
- w_cross_out: bfloat16 [2048, 2048], P('tensor'), may hold values from -0.375 to 0.375
- w_text: bfloat16 [4096, 2048], P(None, 'tensor'), may hold values from -0.09375 to 0.09375
- w_up: bfloat16 [2048, 8192], P(None, 'tensor'), may hold values from -1 to 1
- w_down: bfloat16 [8192, 2048], P('tensor'), may hold values from -0.0625 to 0.0625
- segment_ids: int32 [8, 1024], P('dp'), may hold values from 0 to 3, never falling along the last dimension, each value on 1 to 384 neighbouring positions
- caption_lengths: int32 [32], P('dp'), may hold values from 32 to 128, as said below
Outputs:
- image_out: bfloat16 [8192, 2048], P(('dp', 'tensor'))
- image_grad: bfloat16 [8192, 2048], P(('dp', 'tensor'))
- text_grad: bfloat16 [4096, 4096], P(('dp', 'tensor'))
- gain_grad: float32 [3, 2048], replicated
- shift_grad: float32 [3, 2048], replicated
- self_grad: float32 [3, 2048, 2048], P(None, None, 'tensor')
- self_out_grad: float32 [2048, 2048], P('tensor')
- cross_q_grad: float32 [2048, 2048], P(None, 'tensor')
- cross_kv_grad: float32 [2, 2048, 2048], P(None, None, 'tensor')
- cross_out_grad: float32 [2048, 2048], P('tensor')
- text_w_grad: float32 [4096, 2048], P(None, 'tensor')
- up_grad: float32 [2048, 8192], P(None, 'tensor')
- down_grad: float32 [8192, 2048], P('tensor')
Inputs may be any that keep to these rules, and one draw needn't show every extreme that they name: `segment_ids`: within a row the image number never falls and each of the 4 images has a token; some image has exactly 384 tokens. `caption_lengths`: A caption's live tokens fill the first slots of its 128; some caption is full and some has 32.
All inputs are finite; a program needn't handle non-finite values.
Results may differ from a plain program's by a relative error of at most 0.033.
Values may be sent and summed in bfloat16 or wider, within the bound.
A program may use at most 320 MiB of HBM per device.

v0:
```python
import jax
import jax.numpy as jnp
from jax import lax
from jax.sharding import PartitionSpec as P

HD = 128
IMGS = 4
CAP = 128


epsilon = 1e-05
masked_value = -1e30


def layer_norm(value, gain, shift):
    mean = jnp.mean(value, axis=-1, keepdims=True)
    centered = value - mean
    spread = jnp.mean(centered * centered, axis=-1, keepdims=True)
    return centered * lax.rsqrt(spread + epsilon) * gain + shift


def gelu_tanh(value):
    return jax.nn.gelu(value, approximate=True)


def masked_scores(query, keys, allowed, scale):
    raw = jnp.einsum("bqhe,bkhe->bhqk", query, keys, preferred_element_type=jnp.float32)
    return jnp.where(allowed[:, None], raw * scale, masked_value)


def attend_forward(query, keys, values, allowed, scale):
    scores = masked_scores(query, keys, allowed, scale)
    highest = jnp.max(scores, axis=-1, keepdims=True)
    raised = jnp.exp(scores - highest)
    total = jnp.sum(raised, axis=-1, keepdims=True)
    shares = (raised / total).astype(jnp.bfloat16)
    mixed = jnp.einsum("bhqk,bkhe->bqhe", shares, values, preferred_element_type=jnp.float32)
    return (mixed.astype(jnp.bfloat16), highest + jnp.log(total))


def attend_backward(query, keys, values, allowed, scale, logsum, mixed_back):
    scores = masked_scores(query, keys, allowed, scale)
    shares = jnp.exp(scores - logsum)
    values_back = jnp.einsum(
        "bhqk,bqhe->bkhe",
        shares.astype(jnp.bfloat16),
        mixed_back,
        preferred_element_type=jnp.float32,
    ).astype(jnp.bfloat16)
    shares_back = jnp.einsum(
        "bqhe,bkhe->bhqk", mixed_back, values, preferred_element_type=jnp.float32
    )
    inner = jnp.sum(shares_back * shares, axis=-1, keepdims=True)
    scores_back = (scale * (shares * (shares_back - inner))).astype(jnp.bfloat16)
    query_back = jnp.einsum(
        "bhqk,bkhe->bqhe", scores_back, keys, preferred_element_type=jnp.float32
    ).astype(jnp.bfloat16)
    keys_back = jnp.einsum(
        "bhqk,bqhe->bkhe", scores_back, query, preferred_element_type=jnp.float32
    ).astype(jnp.bfloat16)
    return (query_back, keys_back, values_back)


def local(
    image,
    text,
    cotangent,
    norm_gains,
    norm_shifts,
    w_self,
    w_self_out,
    w_cross_q,
    w_cross_kv,
    w_cross_out,
    w_text,
    w_up,
    w_down,
    segment_ids,
    caption_lengths,
):
    row_count = segment_ids.shape[0]
    local_tokens = image.shape[0]
    width = w_self_out.shape[0]
    local_heads = width // HD
    model_width = w_self.shape[1]
    scale = HD ** (-0.5)
    same_image = segment_ids[:, :, None] == segment_ids[:, None, :]
    slot = jnp.arange(IMGS * CAP, dtype=jnp.int32)
    lengths = caption_lengths.reshape(row_count, IMGS)
    live = (slot % CAP)[None, :] < jnp.repeat(lengths, CAP, axis=1)
    own_caption = segment_ids[:, :, None] == (slot // CAP)[None, None, :]
    cross_allowed = own_caption & live[:, None, :]

    def split_heads(flat):
        return flat.reshape(row_count, -1, local_heads, HD)

    def merge_heads(split):
        return split.reshape(-1, width)

    def normed_tokens(stream, index):
        return layer_norm(stream, norm_gains[index], norm_shifts[index]).astype(jnp.bfloat16)

    def spread(stream, index):
        return lax.all_gather(normed_tokens(stream, index), "tensor", axis=0, tiled=True)

    def respread(stream, index):
        return lax.all_gather(normed_tokens(stream, index), "tensor", axis=0, tiled=True)

    def spread_back(gradient):
        return lax.all_gather(gradient.astype(jnp.bfloat16), "tensor", axis=0, tiled=True)

    def share_rows(left, right):

        def term(start, count):
            return jnp.dot(left, right, preferred_element_type=jnp.float32)

        return lax.psum_scatter(
            term(jnp.int32(0), local_tokens * lax.axis_size("tensor")).astype(jnp.bfloat16),
            "tensor",
            scatter_dimension=0,
            tiled=True,
        ).astype(jnp.float32)

    def share_heads(mixed, w_out):
        return share_rows(mixed, w_out)

    def share_back(pairs):

        def term(start, count):
            total = jnp.zeros((count, model_width), jnp.float32)
            for left, right in pairs:
                total = total + jnp.einsum(
                    "ta,da->td", left, right, preferred_element_type=jnp.float32
                )
            return total

        return lax.psum_scatter(
            term(jnp.int32(0), local_tokens * lax.axis_size("tensor")).astype(jnp.bfloat16),
            "tensor",
            scatter_dimension=0,
            tiled=True,
        ).astype(jnp.float32)

    def norm_back(stream, index, gradient):
        unused, pull = jax.vjp(layer_norm, stream, norm_gains[index], norm_shifts[index])
        return pull(gradient)

    def self_project(whole):
        return jnp.einsum("td,cde->cte", whole, w_self, preferred_element_type=jnp.float32).astype(
            jnp.bfloat16
        )

    def cross_project(whole):
        return jnp.dot(whole, w_cross_q, preferred_element_type=jnp.float32).astype(jnp.bfloat16)

    stream_zero = image.astype(jnp.float32)
    whole_self = spread(stream_zero, 0)
    triple = self_project(whole_self)
    self_mixed, self_logsum = attend_forward(
        split_heads(triple[0]), split_heads(triple[1]), split_heads(triple[2]), same_image, scale
    )
    self_mixed = merge_heads(self_mixed)
    stream_one = stream_zero + share_heads(self_mixed, w_self_out)
    whole_cross = spread(stream_one, 1)
    cross_query = cross_project(whole_cross)
    text_columns = jnp.dot(text, w_text, preferred_element_type=jnp.float32).astype(jnp.bfloat16)
    projected = lax.all_gather(text_columns, "tensor", axis=1, tiled=True)
    text_pair = jnp.einsum(
        "td,cde->cte", projected, w_cross_kv, preferred_element_type=jnp.float32
    ).astype(jnp.bfloat16)
    cross_keys = split_heads(text_pair[0])
    cross_values = split_heads(text_pair[1])
    cross_mixed, cross_logsum = attend_forward(
        split_heads(cross_query), cross_keys, cross_values, cross_allowed, scale
    )
    cross_mixed = merge_heads(cross_mixed)
    stream_two = stream_one + share_heads(cross_mixed, w_cross_out)
    whole_mlp = spread(stream_two, 2)
    hidden = jnp.dot(whole_mlp, w_up, preferred_element_type=jnp.float32)
    active = gelu_tanh(hidden).astype(jnp.bfloat16)
    stream_three = stream_two + share_rows(active, w_down)
    image_out = stream_three.astype(jnp.bfloat16)
    gradient_three = cotangent.astype(jnp.float32)
    mlp_input = respread(stream_two, 2)
    mlp_hidden = jnp.dot(mlp_input, w_up, preferred_element_type=jnp.float32)
    mlp_active = gelu_tanh(mlp_hidden).astype(jnp.bfloat16)
    back_whole = spread_back(gradient_three)
    down_grad = jnp.einsum("tf,td->fd", mlp_active, back_whole, preferred_element_type=jnp.float32)
    active_back = jnp.einsum("td,fd->tf", back_whole, w_down, preferred_element_type=jnp.float32)
    unused, gelu_pull = jax.vjp(gelu_tanh, mlp_hidden)
    hidden_back = gelu_pull(active_back)[0].astype(jnp.bfloat16)
    up_grad = jnp.einsum("td,tf->df", mlp_input, hidden_back, preferred_element_type=jnp.float32)
    stream_back, gain_two, shift_two = norm_back(stream_two, 2, share_back([(hidden_back, w_up)]))
    gradient_two = gradient_three + stream_back
    cross_input = respread(stream_one, 1)
    query_cross = cross_project(cross_input)
    back_whole = spread_back(gradient_two)
    cross_out_grad = jnp.einsum(
        "ta,td->ad", cross_mixed, back_whole, preferred_element_type=jnp.float32
    )
    mixed_back = jnp.einsum(
        "td,ad->ta", back_whole, w_cross_out, preferred_element_type=jnp.float32
    ).astype(jnp.bfloat16)
    query_back, keys_back, values_back = attend_backward(
        split_heads(query_cross),
        cross_keys,
        cross_values,
        cross_allowed,
        scale,
        cross_logsum,
        split_heads(mixed_back),
    )
    query_back = merge_heads(query_back)
    pair_back = jnp.stack([merge_heads(keys_back), merge_heads(values_back)])
    cross_q_grad = jnp.einsum(
        "td,ta->da", cross_input, query_back, preferred_element_type=jnp.float32
    )
    cross_kv_grad = jnp.einsum(
        "td,cta->cda", projected, pair_back, preferred_element_type=jnp.float32
    )
    projected_part = jnp.einsum(
        "cta,cda->td", pair_back, w_cross_kv, preferred_element_type=jnp.float32
    )
    projected_back = lax.psum_scatter(
        projected_part.astype(jnp.bfloat16), "tensor", scatter_dimension=1, tiled=True
    )
    text_w_grad = jnp.einsum("tk,tc->kc", text, projected_back, preferred_element_type=jnp.float32)
    text_grad = lax.psum_scatter(
        jnp.einsum("tc,kc->tk", projected_back, w_text, preferred_element_type=jnp.float32).astype(
            jnp.bfloat16
        ),
        "tensor",
        scatter_dimension=0,
        tiled=True,
    )
    stream_back, gain_one, shift_one = norm_back(
        stream_one, 1, share_back([(query_back, w_cross_q)])
    )
    gradient_one = gradient_two + stream_back
    self_input = respread(stream_zero, 0)
    self_triple = self_project(self_input)
    back_whole = spread_back(gradient_one)
    self_out_grad = jnp.einsum(
        "ta,td->ad", self_mixed, back_whole, preferred_element_type=jnp.float32
    )
    mixed_back = jnp.einsum(
        "td,ad->ta", back_whole, w_self_out, preferred_element_type=jnp.float32
    ).astype(jnp.bfloat16)
    query_back, keys_back, values_back = attend_backward(
        split_heads(self_triple[0]),
        split_heads(self_triple[1]),
        split_heads(self_triple[2]),
        same_image,
        scale,
        self_logsum,
        split_heads(mixed_back),
    )
    triple_back = jnp.stack(
        [merge_heads(query_back), merge_heads(keys_back), merge_heads(values_back)]
    )
    self_grad = jnp.einsum(
        "td,cta->cda", self_input, triple_back, preferred_element_type=jnp.float32
    )
    normed_back = share_back(
        [(triple_back[0], w_self[0]), (triple_back[1], w_self[1]), (triple_back[2], w_self[2])]
    )
    stream_back, gain_zero, shift_zero = norm_back(stream_zero, 0, normed_back)
    image_grad = (gradient_one + stream_back).astype(jnp.bfloat16)
    (
        self_grad,
        self_out_grad,
        cross_q_grad,
        cross_kv_grad,
        cross_out_grad,
        text_w_grad,
        up_grad,
        down_grad,
    ) = (
        lax.psum(self_grad.astype(jnp.bfloat16), "dp").astype(jnp.float32),
        lax.psum(self_out_grad.astype(jnp.bfloat16), "dp").astype(jnp.float32),
        lax.psum(cross_q_grad.astype(jnp.bfloat16), "dp").astype(jnp.float32),
        lax.psum(cross_kv_grad.astype(jnp.bfloat16), "dp").astype(jnp.float32),
        lax.psum(cross_out_grad.astype(jnp.bfloat16), "dp").astype(jnp.float32),
        lax.psum(text_w_grad.astype(jnp.bfloat16), "dp").astype(jnp.float32),
        lax.psum(up_grad.astype(jnp.bfloat16), "dp").astype(jnp.float32),
        lax.psum(down_grad.astype(jnp.bfloat16), "dp").astype(jnp.float32),
    )
    gain_grad = jnp.stack([gain_zero, gain_one, gain_two])
    shift_grad = jnp.stack([shift_zero, shift_one, shift_two])
    gain_grad, shift_grad = lax.psum((gain_grad, shift_grad), ("dp", "tensor"))
    return (
        image_out,
        image_grad,
        text_grad,
        gain_grad,
        shift_grad,
        self_grad,
        self_out_grad,
        cross_q_grad,
        cross_kv_grad,
        cross_out_grad,
        text_w_grad,
        up_grad,
        down_grad,
    )


def solution(mesh):
    placed = (
        P(("dp", "tensor"), None),
        P("dp", None),
        P(("dp", "tensor"), None),
        P(),
        P(),
        P(None, None, "tensor"),
        P("tensor", None),
        P(None, "tensor"),
        P(None, None, "tensor"),
        P("tensor", None),
        P(None, "tensor"),
        P(None, "tensor"),
        P("tensor", None),
        P("dp", None),
        P("dp"),
    )
    return jax.shard_map(
        local,
        mesh=mesh,
        in_specs=placed,
        out_specs=(
            P(("dp", "tensor"), None),
            P(("dp", "tensor"), None),
            P(("dp", "tensor"), None),
            P(),
            P(),
            P(None, None, "tensor"),
            P("tensor", None),
            P(None, "tensor"),
            P(None, None, "tensor"),
            P("tensor", None),
            P(None, "tensor"),
            P(None, "tensor"),
            P("tensor", None),
        ),
        check_vma=False,
    )
```

profile of v0, /device:TPU:0, one launch (start us, length us, event | category | flops | bytes accessed | tf_op | source)
XLA Modules:
  0.0 1856.8 jit_solution(15552894290457365440)
XLA Ops:
  18.7 81.8 %all-gather.8.cloned.1.call-done = bf16[2048,2048]{1,0:T(8,128)(2,1)} async-done(((bf16[256,2048]{1,0:T(8,128)(2,1)}), bf16[2048,2048]{1,0:T(8,128)(2,1)}) %all-gather.8.cloned.1.call-update) | async-done | bytes 8388624 | tf_op jit(solution)/shard_map/all_gather | solution.py:104
  100.5 10.0 fusion.105
  121.9 3.7 copy.76
  125.6 5.8 fusion.4
  131.4 4.0 fusion.3
  138.1 6.5 fusion.161
  147.4 7.4 convolution_convert_fusion.5
  154.8 6.6 convolution_convert_fusion.15
  161.5 81.6 %reduce-scatter.9.cloned.1.call-done = bf16[256,2048]{1,0:T(8,128)(2,1)} async-done(((bf16[2048,2048]{1,0:T(8,128)(2,1)}), bf16[256,2048]{1,0:T(8,128)(2,1)}) %reduce-scatter.9.cloned.1.call-update) | async-done | bytes 1048592 | tf_op jit(solution)/shard_map/reduce_scatter | solution.py:117
  251.1 40.3 %all-gather.10.cloned.1.call-done = bf16[1024,2048]{1,0:T(8,128)(2,1)} async-done(((bf16[1024,256]{1,0:T(8,128)(2,1)}), bf16[1024,2048]{1,0:T(8,128)(2,1)}) %all-gather.10.cloned.1.call-update) | async-done | bytes 4194320 | tf_op jit(solution)/shard_map/all_gather | solution.py:167
  291.4 5.2 fusion.148
  303.7 70.1 %all-gather.12.cloned.1.call-done = bf16[2048,2048]{1,0:T(8,128)(2,1)} async-done(((bf16[256,2048]{1,0:T(8,128)(2,1)}), bf16[2048,2048]{1,0:T(8,128)(2,1)}) %all-gather.12.cloned.1.call-update) | async-done | bytes 8388624 | tf_op jit(solution)/shard_map/all_gather | solution.py:104
  373.7 6.9 convolution_convert_fusion.14
  386.5 3.8 fusion.47
  393.5 3.8 fusion.151
  397.3 3.7 copy.65
  401.0 7.3 convolution_convert_fusion.4
  408.9 87.7 %reduce-scatter.11.cloned.1.call-done = bf16[256,2048]{1,0:T(8,128)(2,1)} async-done(((bf16[2048,2048]{1,0:T(8,128)(2,1)}), bf16[256,2048]{1,0:T(8,128)(2,1)}) %reduce-scatter.11.cloned.1.call-update) | async-done | bytes 1048592 | tf_op jit(solution)/shard_map/reduce_scatter | solution.py:117
  501.4 77.0 %all-gather.16.cloned.1.call-done = bf16[2048,2048]{1,0:T(8,128)(2,1)} async-done(((bf16[256,2048]{1,0:T(8,128)(2,1)}), bf16[2048,2048]{1,0:T(8,128)(2,1)}) %all-gather.16.cloned.1.call-update) | async-done | bytes 8388624 | tf_op jit(solution)/shard_map/all_gather | solution.py:110
  578.5 23.7 %fusion.255 = f32[2048,1024]{1,0:T(8,128)} fusion(bf16[2048,2048]{1,0:T(8,128)(2,1)} %all-gather.16.cloned.1.call-done, bf16[1024,2048]{1,0:T(8,128)(2,1)} %param.27), kind=kOutput, calls=%fused_computation.258 | convolution fusion | flops 8589934592 | bytes 20971520 | tf_op jit(solution)/shard_map/td,fd->tf/dot_general | solution.py:189
  602.2 59.1 %all-gather.14.cloned.1.call-done = bf16[2048,2048]{1,0:T(8,128)(2,1)} async-done(((bf16[256,2048]{1,0:T(8,128)(2,1)}), bf16[2048,2048]{1,0:T(8,128)(2,1)}) %all-gather.14.cloned.1.call-update) | async-done | bytes 8388624 | tf_op jit(solution)/shard_map/all_gather | solution.py:104
  661.3 22.3 %fusion.20 = (bf16[2048,1024]{1,0:T(8,128)(2,1)S(1)}, f32[2048,1024]{1,0:T(8,128)}) fusion(f32[2048,1024]{1,0:T(8,128)} %fusion.255, bf16[2048,2048]{1,0:T(8,128)(2,1)} %all-gather.14.cloned.1.call-done, bf16[2048,1024]{1,0:T(8,128)(2,1)} %param.26), kind=kOutput, calls=%fused_computation.23 | convolution fusion | flops 8631877632 | bytes 33554432 | tf_op jit(solution)/shard_map/dot_general | solution.py:179
  685.6 10.9 convolution_convert_fusion.2
  696.6 15.3 convolution_convert_fusion.3
  711.9 72.9 %reduce-scatter.15.cloned.1.call-done = bf16[256,2048]{1,0:T(8,128)(2,1)} async-done(((bf16[2048,2048]{1,0:T(8,128)(2,1)}), bf16[256,2048]{1,0:T(8,128)(2,1)}) %reduce-scatter.15.cloned.1.call-update) | async-done | bytes 1048592 | tf_op jit(solution)/shard_map/reduce_scatter | solution.py:137
  788.1 87.0 %reduce-scatter.13.cloned.1.call-done = bf16[256,2048]{1,0:T(8,128)(2,1)} async-done(((bf16[2048,2048]{1,0:T(8,128)(2,1)}), bf16[256,2048]{1,0:T(8,128)(2,1)}) %reduce-scatter.13.cloned.1.call-update) | async-done | bytes 1048592 | tf_op jit(solution)/shard_map/reduce_scatter | solution.py:117
  875.1 3.9 fusion.249
  883.0 80.5 %all-gather.18.cloned.1.call-done = bf16[2048,2048]{1,0:T(8,128)(2,1)} async-done(((bf16[256,2048]{1,0:T(8,128)(2,1)}), bf16[2048,2048]{1,0:T(8,128)(2,1)}) %all-gather.18.cloned.1.call-update) | async-done | bytes 8388624 | tf_op jit(solution)/shard_map/all_gather | solution.py:110
  963.5 7.0 convolution_convert_fusion.13
  976.6 6.0 fusion.206
  982.6 15.4 fusion.145
  998.0 3.7 copy.70
  1001.7 7.2 convolution_convert_fusion.1
  1008.9 88.3 %reduce-scatter.17.cloned.1.call-done = bf16[256,2048]{1,0:T(8,128)(2,1)} async-done(((bf16[2048,2048]{1,0:T(8,128)(2,1)}), bf16[256,2048]{1,0:T(8,128)(2,1)}) %reduce-scatter.17.cloned.1.call-update) | async-done | bytes 1048592 | tf_op jit(solution)/shard_map/reduce_scatter | solution.py:137
  1103.4 5.3 fusion.248
  1109.0 7.4 fusion.173
  1120.7 14.4 fusion.170
  1138.8 6.1 bitcast_convert_fusion
  1145.1 44.3 %all-gather.20.cloned.1.call-done = bf16[2048,2048]{1,0:T(8,128)(2,1)} async-done(((bf16[256,2048]{1,0:T(8,128)(2,1)}), bf16[2048,2048]{1,0:T(8,128)(2,1)}) %all-gather.20.cloned.1.call-update) | async-done | bytes 8388624 | tf_op jit(solution)/shard_map/all_gather | solution.py:110
  1189.3 6.7 convolution_convert_fusion.12
  1199.7 10.2 fusion.158
  1209.9 3.7 copy.81
  1213.6 9.3 fusion.203
  1222.9 26.1 %fusion.152 = bf16[2,1024,2,128]{1,3,2,0:T(8,128)(2,1)S(1)} fusion(bf16[2,1024,2,128]{1,3,2,0:T(8,128)(2,1)} %copy.76, f32[2,2,1024,1024]{2,3,1,0:T(8,128)} %fusion.203, f32[2,2,1024,1024]{2,3,1,0:T(8,128)} %copy-done.6, f32[2,2,1024]{2,1,0:T(2,128)S(1)} %log_add_fusion, pred[2,1024,1024]{1,2,0:T(8,128)(4,1)} %broadcast_compare_fusion), kind=kOutput, calls=%fused_computation.152 | convolution fusion | flops 1120408576 | bytes 37765120 | tf_op jit(solution)/shard_map/bhqk,bqhe->bkhe/dot_general | solution.py:58
  1251.1 25.9 %fusion.155 = bf16[2,1024,2,128]{1,3,2,0:T(8,128)(2,1)} fusion(bf16[2,1024,2,128]{1,3,2,0:T(8,128)(2,1)} %copy.73, f32[2,2,1024,1024]{2,3,1,0:T(8,128)} %fusion.203, f32[2,2,1024,1024]{2,3,1,0:T(8,128)} %copy-done.6, f32[2,2,1024]{2,1,0:T(2,128)S(1)} %log_add_fusion, pred[2,1024,1024]{1,2,0:T(8,128)(4,1)} %broadcast_compare_fusion), kind=kOutput, calls=%fused_computation.153 | convolution fusion | flops 1120408576 | bytes 37765120 | tf_op jit(solution)/shard_map/bhqk,bkhe->bqhe/dot_general | solution.py:55
  1280.0 9.4 fusion.181
  1289.4 9.4 fusion.178
  1298.8 15.7 add_convert_fusion
  1314.6 14.0 convolution_convert_fusion.8
  1328.6 16.5 convolution_convert_fusion.7
  1345.1 3.7 fusion.108
  1348.8 6.9 convolution_convert_fusion.9
  1359.4 7.5 fusion.50
  1381.1 6.9 convolution_convert_fusion.11
  1388.0 10.3 fusion.97
  1398.4 6.8 convolution_convert_fusion
  1409.6 40.4 %all-reduce = (f32[3,2048]{1,0:T(4,128)}, f32[3,2048]{1,0:T(4,128)}) all-reduce(f32[3,2048]{1,0:T(4,128)S(1)} %get-tuple-element.84, f32[3,2048]{1,0:T(4,128)S(1)} %get-tuple-element.85), channel_id=1, replica_groups=mesh['dp'=4,'tensor'=8] {'dp','tensor'}, use_global_device_ids=true, to_apply=%region_29.30 | all-reduce | flops 12288 | bytes 98304 | tf_op jit(solution)/shard_map/psum | solution.py:290
  1453.6 302.4 %all-reduce.4.cloned.1.call-done = (bf16[3,2048,256]{1,2,0:T(8,128)(2,1)}, bf16[2,2048,256]{1,2,0:T(8,128)(2,1)}, bf16[4096,256]{0,1:T(8,128)(2,1)}, bf16[256,20...) async-done(((bf16[3,2048,256]{1,2,0:T(8,128)(2,1)}, ...) | async-done | bytes 18874384 | tf_op jit(solution)/shard_map/psum | solution.py:279
  1764.3 5.5 copy.95
  1769.8 4.1 copy.96
  1773.9 4.3 copy.97
  1778.2 6.9 convert_element_type.300
  1785.1 4.4 convert_element_type.302
  1789.5 60.3 %reduce-scatter.23.cloned.1.call-done = bf16[128,4096]{1,0:T(8,128)(2,1)} async-done(((bf16[1024,4096]{1,0:T(8,128)(2,1)}), bf16[128,4096]{1,0:T(8,128)(2,1)}) %reduce-scatter.23.cloned.1.call-update) | async-done | bytes 1048592 | tf_op jit(solution)/shard_map/reduce_scatter | solution.py:228
  (232 shorter events, 130.8 us)
Async XLA Ops:
  7.2 147.7 %copy-start = (bf16[4096,256]{1,0:T(8,128)(2,1)S(1)}, bf16[4096,256]{1,0:T(8,128)(2,1)}, u32[]{:S(2)}) copy-start(bf16[4096,256]{1,0:T(8,128)(2,1)} %param.25) | copy-start | bytes 6291460
  7.2 93.3 %all-gather.8.cloned.1.call-start = ((), (), s32[]{:S(2)}) async-start(), calls=%async_computation.8 | async-start | bytes 9437184 | tf_op jit(solution)/shard_map/all_gather | solution.py:104
  8.8 101.7 %copy-start.39 = (f32[256]{0:T(256)}, f32[256]{0:T(256)S(1)}, u32[]{:S(2)}) copy-start(f32[256]{0:T(256)S(1)} %broadcast_multiply_fusion.2) | copy-start | bytes 3076
  11.1 99.5 %copy-start.47 = (f32[256]{0:T(256)}, f32[256]{0:T(256)S(1)}, u32[]{:S(2)}) copy-start(f32[256]{0:T(256)S(1)} %fusion.215) | copy-start | bytes 3076
  12.0 234.4 %copy-start.32 = (f32[1,2048]{1,0:T(1,128)}, f32[1,2048]{1,0:T(1,128)S(1)}, u32[]{:S(2)}) copy-start(f32[1,2048]{1,0:T(1,128)S(1)} %get-tuple-element.74) | copy-start | bytes 24580
  15.6 227.5 %reduce-scatter.9.cloned.1.call-start = ((), (), s32[]{:S(2)}) async-start(), calls=%async_computation.9 | async-start | bytes 9437184 | tf_op jit(solution)/shard_map/reduce_scatter | solution.py:117
  113.6 21.8 %copy-start.14 = (bf16[2,1024,2,128]{3,2,1,0:T(2,128)(2,1)}, bf16[2,1024,2,128]{3,2,1,0:T(2,128)(2,1)S(1)}, u32[]{:S(2)}) copy-start(bf16[2,1024,2,128]{3,2,1,0:T(2,128)(2,1)S(1)} %reshape_squeeze.18) | copy-start | bytes 3145732
  125.6 5.9 copy-start.11
  131.4 5.7 copy-start.6
  131.4 6.1 copy-start.35
  147.4 7.4 copy-start.7
  154.7 88.3 %copy-start.1 = (bf16[256,2048]{1,0:T(8,128)(2,1)S(1)}, bf16[256,2048]{1,0:T(8,128)(2,1)}, u32[]{:S(2)}) copy-start(bf16[256,2048]{1,0:T(8,128)(2,1)} %param.15) | copy-start | bytes 3145732
  154.8 94.5 %copy-start.57 = (s32[8]{0:T(128)S(1)}, s32[8]{0:T(128)}, u32[]{:S(2)}) copy-start(s32[8]{0:T(128)} %param.29) | copy-start | bytes 100
  154.8 94.7 %copy-start.34 = (s32[2,1024]{1,0:T(2,128)S(1)}, s32[2,1024]{1,0:T(2,128)}, u32[]{:S(2)}) copy-start(s32[2,1024]{1,0:T(2,128)} %param.28) | copy-start | bytes 24580
  154.8 136.6 %all-gather.10.cloned.1.call-start = ((), (), s32[]{:S(2)}) async-start(), calls=%async_computation.10 | async-start | bytes 4718592 | tf_op jit(solution)/shard_map/all_gather | solution.py:167
  161.4 212.3 %all-gather.12.cloned.1.call-start = ((), (), s32[]{:S(2)}) async-start(), calls=%async_computation.11 | async-start | bytes 9437184 | tf_op jit(solution)/shard_map/all_gather | solution.py:104
  246.4 50.2 %copy-start.51 = (f32[256]{0:T(256)}, f32[256]{0:T(256)S(1)}, u32[]{:S(2)}) copy-start(f32[256]{0:T(256)S(1)} %multiply_reduce_fusion.3) | copy-start | bytes 3076
  246.4 50.2 %copy-start.49 = (f32[256]{0:T(256)}, f32[256]{0:T(256)S(1)}, u32[]{:S(2)}) copy-start(f32[256]{0:T(256)S(1)} %fusion.216) | copy-start | bytes 3076
  249.2 247.4 %reduce-scatter.11.cloned.1.call-start = ((), (), s32[]{:S(2)}) async-start(), calls=%async_computation.12 | async-start | bytes 9437184 | tf_op jit(solution)/shard_map/reduce_scatter | solution.py:117
  386.5 3.8 copy-start.10
  386.5 7.1 copy-start.23
  408.3 170.2 %all-gather.16.cloned.1.call-start = ((), (), s32[]{:S(2)}) async-start(), calls=%async_computation.15 | async-start | bytes 9437184 | tf_op jit(solution)/shard_map/all_gather | solution.py:110
  408.9 252.4 %all-gather.14.cloned.1.call-start = ((), (), s32[]{:S(2)}) async-start(), calls=%async_computation.13 | async-start | bytes 9437184 | tf_op jit(solution)/shard_map/all_gather | solution.py:104
  501.4 283.5 %reduce-scatter.15.cloned.1.call-start = ((), (), s32[]{:S(2)}) async-start(), calls=%async_computation.16 | async-start | bytes 9437184 | tf_op jit(solution)/shard_map/reduce_scatter | solution.py:137
  661.3 24.3 %copy-start.55 = (bf16[2048,1024]{1,0:T(8,128)(2,1)S(1)}, bf16[2048,1024]{1,0:T(8,128)(2,1)}, u32[]{:S(2)}) copy-start(bf16[2048,1024]{1,0:T(8,128)(2,1)} %param.26) | copy-start | bytes 12582916
  696.5 178.6 %reduce-scatter.13.cloned.1.call-start = ((), (), s32[]{:S(2)}) async-start(), calls=%async_computation.14 | async-start | bytes 9437184 | tf_op jit(solution)/shard_map/reduce_scatter | solution.py:117
  711.9 251.6 %all-gather.18.cloned.1.call-start = ((), (), s32[]{:S(2)}) async-start(), calls=%async_computation.17 | async-start | bytes 9437184 | tf_op jit(solution)/shard_map/all_gather | solution.py:110
  882.9 214.3 %reduce-scatter.17.cloned.1.call-start = ((), (), s32[]{:S(2)}) async-start(), calls=%async_computation.18 | async-start | bytes 9437184 | tf_op jit(solution)/shard_map/reduce_scatter | solution.py:137
  1001.7 95.5 %copy-start.33 = (f32[1,2048]{1,0:T(1,128)S(1)}, f32[1,2048]{1,0:T(1,128)}, u32[]{:S(2)}) copy-start(f32[1,2048]{1,0:T(1,128)} %copy-done.32) | copy-start | bytes 24580
  1001.7 95.5 %copy-start.42 = (f32[256]{0:T(256)S(1)}, f32[256]{0:T(256)}, u32[]{:S(2)}) copy-start(f32[256]{0:T(256)} %copy-done.41) | copy-start | bytes 3076
  1008.9 91.3 %copy-start.52 = (f32[256]{0:T(256)S(1)}, f32[256]{0:T(256)}, u32[]{:S(2)}) copy-start(f32[256]{0:T(256)} %copy-done.51) | copy-start | bytes 3076
  1008.9 91.3 %copy-start.50 = (f32[256]{0:T(256)S(1)}, f32[256]{0:T(256)}, u32[]{:S(2)}) copy-start(f32[256]{0:T(256)} %copy-done.49) | copy-start | bytes 3076
  1008.9 180.4 %all-gather.20.cloned.1.call-start = ((), (), s32[]{:S(2)}) async-start(), calls=%async_computation.19 | async-start | bytes 9437184 | tf_op jit(solution)/shard_map/all_gather | solution.py:110
  1108.8 11.9 copy-start.22
  1108.8 250.6 %reduce-scatter.21.cloned.1.call-start = ((), (), s32[]{:S(2)}) async-start(), calls=%async_computation.21 | async-start | bytes 4718592 | tf_op jit(solution)/shard_map/reduce_scatter | solution.py:224
  1138.8 6.2 copy-start.36
  1138.8 6.2 copy-start.38
  1138.8 50.5 %copy-start.27 = (bf16[256,2048]{1,0:T(8,128)(2,1)S(1)}, bf16[256,2048]{1,0:T(8,128)(2,1)}, u32[]{:S(2)}) copy-start(bf16[256,2048]{1,0:T(8,128)(2,1)} %param.21) | copy-start | bytes 3145732
  1145.0 260.3 %reduce-scatter.19.cloned.1.call-start = ((), (), s32[]{:S(2)}) async-start(), calls=%async_computation.20 | async-start | bytes 9437184 | tf_op jit(solution)/shard_map/reduce_scatter | solution.py:137
  1199.7 13.9 copy-start.15
  1280.0 9.4 copy-start.17
  1289.4 9.4 copy-start.16
  1314.5 441.4 %all-reduce.4.cloned.1.call-start = ((), (), s32[]{:S(2)}) async-start(), calls=%async_computation.23 | async-start | bytes 37748736 | tf_op jit(solution)/shard_map/psum | solution.py:279
  1328.6 16.5 copy-start.29
  1328.6 16.5 copy-start.56
  1345.1 10.6 slice-start
  1348.8 6.9 copy-start.12
  1348.8 6.9 slice-start.1
  1359.4 7.5 copy-start.18
  1359.4 9.5 copy-start.20
  1359.4 11.6 copy-start.21
  1366.9 14.2 copy-start.8
  1381.1 7.0 copy-start.24
  1381.1 7.0 copy-start.25
  1381.1 7.0 copy-start.26
  1398.3 6.9 copy-start.2
  1398.4 6.9 copy-start.31
  1398.4 6.9 copy-start.40
  1398.4 451.5 %reduce-scatter.23.cloned.1.call-start = ((), (), s32[]{:S(2)}) async-start(), calls=%async_computation.22 | async-start | bytes 9437184 | tf_op jit(solution)/shard_map/reduce_scatter | solution.py:228
  1405.2 4.3 copy-start.43
  1405.2 4.3 copy-start.44
  1405.2 4.3 copy-start.45
  1405.2 4.3 copy-start.46
  1778.2 6.9 copy-start.13
  (13 other events, 22.7 us)
Sparse Core Ops, SparseCore 0:
  15.7 84.7 all-gather.7
  154.9 88.1 reduce-scatter.8
  245.2 46.1 all-gather.9
  293.4 80.2 all-gather.11
  408.4 88.1 reduce-scatter.10
  498.0 80.3 all-gather.15
  580.6 80.5 all-gather.13
  696.7 88.1 reduce-scatter.14
  787.1 87.9 reduce-scatter.12
  883.0 80.3 all-gather.17
  1009.0 88.1 reduce-scatter.16
  1108.9 80.3 all-gather.19
  1192.2 48.5 reduce-scatter.20
  1314.7 87.9 reduce-scatter.18
  1408.4 347.5 all-reduce.3
  1758.8 90.9 reduce-scatter.22
where the time goes:
time: 1870 us; the launch traced here: 1860 us
  waiting for transfers between devices  1230 us (66%)
  matrix products  388 us (21%)
  local copies, waits for them, and re-layouts  103 us (6%)
  other arithmetic  75.2 us (4%)
  blocking collectives  40.4 us (2%)
    psum x1, waiting for transfers between devices, local(): lax.psum(self_grad.astype(jnp.bfloat16), 'dp').astype(jnp.float32)  302 us
    reduce_scatter x3, waiting for transfers between devices, share_rows(): lax.psum_scatter(term(jnp.int32(0), local_tokens * lax.axis_size('tensor'...  256 us
    all_gather x3, waiting for transfers between devices, spread(): lax.all_gather(normed_tokens(stream, index), 'tensor', axis=0, tiled=True)  211 us
    all_gather x3, waiting for transfers between devices, spread_back(): lax.all_gather(gradient.astype(jnp.bfloat16), 'tensor', axis=0, tiled=True)  202 us
    reduce_scatter x3, waiting for transfers between devices, share_back(): lax.psum_scatter(term(jnp.int32(0), local_tokens * lax.axis_size('tensor'...  161 us
    reduce_scatter x1, waiting for transfers between devices, local(): lax.psum_scatter(jnp.einsum('tc,kc->tk', projected_back, w_text, preferre...  60.3 us
    dot_general x5, matrix products, term(): jnp.einsum('ta,da->td', left, right, preferred_element_type=jnp.float32)  52.6 us
    dot_general x2, matrix products, attend_backward(): jnp.einsum('bhqk,bkhe->bqhe', scores_back, keys, preferred_element_type=j...  41.3 us
  transfers between devices with their start and end apart: 16, of which 14 were waited for; matrix products, arithmetic and copies ran while one was open for 20% of the time, Pallas kernels for 0%

commit v1 on v0

v1 whole, which is shorter than its diff:
```python
import functools

import jax
import jax.numpy as jnp
from jax import lax
from jax.experimental import pallas as pl
from jax.experimental.pallas import tpu as pltpu
from jax.sharding import PartitionSpec as P

HD = 128
IMGS = 4
CAP = 128
SCALE = HD ** (-0.5)
MIB = 1024 * 1024

epsilon = 1e-05
masked_value = -1e30

TENSOR = "tensor"
DP = "dp"

F32 = jnp.float32
BF16 = jnp.bfloat16


def shares_of(q, k, allowed):
    raw = lax.dot_general(q, k, (((1,), (1,)), ((), ())), preferred_element_type=F32)
    scores = jnp.where(allowed, raw * SCALE, masked_value)
    highest = jnp.max(scores, axis=-1, keepdims=True)
    raised = jnp.exp(scores - highest)
    return raised * (1.0 / jnp.sum(raised, axis=-1, keepdims=True))


def attend_kernel(step, qid_ref, kid_ref, q_ref, k_ref, v_ref, o_ref):
    k = k_ref[...]
    v = v_ref[...]
    kid = kid_ref[...]
    for start in range(0, q_ref.shape[0], step):
        rows = pl.ds(start, step)
        shares = shares_of(q_ref[rows, :], k, qid_ref[rows, :] == kid)
        mixed = jnp.dot(shares.astype(BF16), v, preferred_element_type=F32)
        o_ref[rows, :] = mixed.astype(BF16)


def attend_back_kernel(step, qid_ref, kid_ref, q_ref, k_ref, v_ref, do_ref, dq_ref, dk_ref, dv_ref, dk_sum, dv_sum):
    k = k_ref[...]
    v = v_ref[...]
    kid = kid_ref[...]
    for start in range(0, q_ref.shape[0], step):
        rows = pl.ds(start, step)
        q = q_ref[rows, :]
        do = do_ref[rows, :]
        shares = shares_of(q, k, qid_ref[rows, :] == kid)
        dp = lax.dot_general(do, v, (((1,), (1,)), ((), ())), preferred_element_type=F32)
        inner = jnp.sum(dp * shares, axis=-1, keepdims=True)
        ds = (SCALE * (shares * (dp - inner))).astype(BF16)
        dq_ref[rows, :] = jnp.dot(ds, k, preferred_element_type=F32).astype(BF16)
        dk = lax.dot_general(ds, q, (((0,), (0,)), ((), ())), preferred_element_type=F32)
        dv = lax.dot_general(
            shares.astype(BF16), do, (((0,), (0,)), ((), ())), preferred_element_type=F32
        )
        if start == 0:
            dk_sum[...] = dk
            dv_sum[...] = dv
        else:
            dk_sum[...] += dk
            dv_sum[...] += dv
    dk_ref[...] = dk_sum[...].astype(BF16)
    dv_ref[...] = dv_sum[...].astype(BF16)


def head_spec(rows, which):
    if which is None:
        return pl.BlockSpec((rows, HD), lambda h: (0, h))
    return pl.BlockSpec((None, rows, HD), lambda h: (which, 0, h))


def whole_spec(shape):
    return pl.BlockSpec(shape, lambda h: (0, 0))


def attend(qid, kid, query, keys, values):
    (qa, qp), (ka, kp), (va, vp) = query, keys, values
    tokens, width = qa.shape[-2:]
    slots = ka.shape[-2]
    heads = width // HD
    return pl.pallas_call(
        functools.partial(attend_kernel, 256),
        grid=(heads,),
        in_specs=[
            whole_spec(qid.shape),
            whole_spec(kid.shape),
            head_spec(tokens, qp),
            head_spec(slots, kp),
            head_spec(slots, vp),
        ],
        out_specs=head_spec(tokens, None),
        out_shape=jax.ShapeDtypeStruct((tokens, width), BF16),
        compiler_params=pltpu.CompilerParams(vmem_limit_bytes=48 * MIB),
        cost_estimate=pl.CostEstimate(
            flops=4 * tokens * slots * width,
            bytes_accessed=2 * width * (2 * tokens + 2 * slots),
            transcendentals=tokens * slots * heads,
        ),
        name="attend",
    )(qid, kid, qa, ka, va)


def attend_back(qid, kid, query, keys, values, do):
    (qa, qp), (ka, kp), (va, vp) = query, keys, values
    tokens, width = qa.shape[-2:]
    slots = ka.shape[-2]
    heads = width // HD
    return pl.pallas_call(
        functools.partial(attend_back_kernel, 256),
        grid=(heads,),
        in_specs=[
            whole_spec(qid.shape),
            whole_spec(kid.shape),
            head_spec(tokens, qp),
            head_spec(slots, kp),
            head_spec(slots, vp),
            head_spec(tokens, None),
        ],
        out_specs=[head_spec(tokens, None), head_spec(slots, None), head_spec(slots, None)],
        out_shape=[
            jax.ShapeDtypeStruct((tokens, width), BF16),
            jax.ShapeDtypeStruct((slots, width), BF16),
            jax.ShapeDtypeStruct((slots, width), BF16),
        ],
        scratch_shapes=[pltpu.VMEM((slots, HD), F32), pltpu.VMEM((slots, HD), F32)],
        compiler_params=pltpu.CompilerParams(vmem_limit_bytes=48 * MIB),
        cost_estimate=pl.CostEstimate(
            flops=10 * tokens * slots * width,
            bytes_accessed=2 * width * (3 * tokens + 4 * slots),
            transcendentals=tokens * slots * heads,
        ),
        name="attend_back",
    )(qid, kid, qa, ka, va, do)


def dot(left, right):
    return jnp.dot(left, right, preferred_element_type=F32)


def dot_t(left, right):
    return lax.dot_general(left, right, (((0,), (0,)), ((), ())), preferred_element_type=F32)


def dot_r(left, right):
    return lax.dot_general(left, right, (((1,), (1,)), ((), ())), preferred_element_type=F32)


def planes_of(left, right):
    return jnp.einsum("td,cde->cte", left, right, preferred_element_type=F32).astype(BF16)


def planes_grad(left, right):
    return jnp.einsum("td,cta->cda", left, right, preferred_element_type=F32).astype(BF16)


def planes_back(left, right):
    return jnp.einsum("cta,cda->td", left, right, preferred_element_type=F32).astype(BF16)


def norm_parts(value):
    mean = jnp.mean(value, axis=-1, keepdims=True)
    centered = value - mean
    spread = jnp.mean(centered * centered, axis=-1, keepdims=True)
    rate = lax.rsqrt(spread + epsilon)
    return centered * rate, rate


def gelu_parts(h):
    c = 0.7978845608028654
    inner = c * (h + 0.044715 * h * h * h)
    th = jnp.tanh(inner)
    half = 0.5 * (1.0 + th)
    slope = half + 0.5 * h * (1.0 - th * th) * (c * (1.0 + 3 * 0.044715 * h * h))
    return h * half, slope


def partner(index, bit):
    return index + bit - 2 * bit * ((index // bit) % 2)


def peer(index, mask):
    bit = 1
    while bit <= mask:
        if mask & bit:
            index = partner(index, bit)
        bit *= 2
    return index


def low_bit(value):
    return value & -value


def high_bit(value):
    return 1 << (value.bit_length() - 1)


def level_of(value):
    return sum((value >> i) & 1 for i in range(value.bit_length()))


def bits_of(size):
    return tuple(1 << i for i in range(size.bit_length() - 1))


def remote(src, dst, send_sem, recv_sem, axis, index):
    copy = pltpu.make_async_remote_copy(
        src_ref=src,
        dst_ref=dst,
        send_sem=send_sem,
        recv_sem=recv_sem,
        device_id={axis: index},
        device_id_type=pl.DeviceIdType.MESH,
    )
    copy.start()
    return copy


def local_copy(src, dst, sem):
    copy = pltpu.make_async_copy(src, dst, sem)
    copy.start()
    return copy


VMEM = pl.BlockSpec(memory_space=pltpu.VMEM)
HBM = pl.BlockSpec(memory_space=pl.ANY)
DMA = pltpu.SemaphoreType.DMA


class Flow:
    def __init__(self, partners):
        self.partners = partners
        self.ins, self.outs, self.scratch = [], [], []
        self.steps = None

    def take(self, array, spec=HBM):
        self.ins.append((array, spec))
        return (0, len(self.ins) - 1)

    def give(self, shape, dtype, spec=HBM):
        self.outs.append((jax.ShapeDtypeStruct(shape, dtype), spec))
        return (1, len(self.outs) - 1)

    def hold(self, kind):
        self.scratch.append((kind, None))
        return (2, len(self.scratch) - 1)

    def vmem(self, *shape, dtype=BF16):
        return self.hold(pltpu.VMEM(shape, dtype))

    def sems(self, *shape):
        return self.hold(DMA(shape))


def flows_kernel(flows, *refs):
    refs = list(refs)
    tables = [{} for unused in flows]
    for part in range(3):
        for flow, table in zip(flows, tables):
            for i in range(len((flow.ins, flow.outs, flow.scratch)[part])):
                table[part, i] = refs.pop(0)
    partners = []
    for flow in flows:
        partners += [entry for entry in flow.partners if entry not in partners]
    barrier = pltpu.get_barrier_semaphore()
    for axis, bit in partners:
        pl.semaphore_signal(
            barrier,
            inc=1,
            device_id={axis: partner(lax.axis_index(axis), bit)},
            device_id_type=pl.DeviceIdType.MESH,
        )
    pl.semaphore_wait(barrier, len(partners))
    running = [[0.0, flow.steps(table)] for flow, table in zip(flows, tables)]
    while running:
        entry = min(running, key=lambda e: e[0])
        moment = next(entry[1], None)
        if moment is None:
            running.remove(entry)
        else:
            entry[0] = moment


def run_flows(cid, name, micros, *flows):
    ins, outs, scratch = [
        [entry for flow in flows for entry in part(flow)]
        for part in (lambda f: f.ins, lambda f: f.outs, lambda f: f.scratch)
    ]
    results = pl.pallas_call(
        functools.partial(flows_kernel, flows),
        in_specs=[entry[1] for entry in ins],
        out_specs=[entry[1] for entry in outs],
        out_shape=[entry[0] for entry in outs],
        scratch_shapes=[entry[0] for entry in scratch],
        compiler_params=pltpu.CompilerParams(
            collective_id=cid, has_side_effects=True, vmem_limit_bytes=58 * MIB
        ),
        cost_estimate=pl.CostEstimate(
            flops=0, bytes_accessed=int(micros * 3.3e6), transcendentals=0
        ),
        name=name,
    )(*[entry[0] for entry in ins])
    results = list(results)
    return [tuple(results.pop(0) for unused in flow.outs) for flow in flows]


class Sum:
    def __init__(self, flow, size, chunks, high, wide):
        self.size, self.chunks = size, chunks
        self.held = flow.vmem(size // 2, high, wide)
        self.came = flow.vmem(size - 1, high, wide)
        self.load = flow.sems(size // 2, chunks)
        self.sent = flow.sems(size, chunks)
        self.got = flow.sems(size, chunks)

    def steps(self, r, view, rows, finish, clock):
        bits = bits_of(self.size)
        chunks = self.chunks
        index = lax.axis_index(TENSOR)
        held, came = r[self.held], r[self.came]
        firsts = sorted(range(0, self.size, 2), reverse=True)
        sent, loads = {}, {}

        def send(src, block, chunk, bit):
            sent[block, chunk] = remote(
                src,
                came.at[block - 1, rows(chunk)],
                r[self.sent].at[block, chunk],
                r[self.got].at[block, chunk],
                TENSOR,
                partner(index, bit),
            )

        def summed(block, chunk):
            loads[block, chunk].wait()
            total = held[block // 2, rows(chunk)].astype(F32)
            for bit in bits:
                if block == 0 or bit < low_bit(block):
                    sent[block + bit, chunk].wait_recv()
                    total = total + came[block + bit - 1, rows(chunk)].astype(F32)
            return total

        for block in firsts:
            for chunk in range(chunks):
                send(view(block + 1, chunk), block + 1, chunk, 1)
                loads[block, chunk] = local_copy(
                    view(block, chunk),
                    held.at[block // 2, rows(chunk)],
                    r[self.load].at[block // 2, chunk],
                )
        start, middle, pace, last = clock
        yield start
        for block in firsts:
            if block:
                for chunk in range(chunks):
                    if low_bit(block) > 2:
                        yield middle + chunk * pace
                    held[block // 2, rows(chunk)] = summed(block, chunk).astype(BF16)
                    send(held.at[block // 2, rows(chunk)], block, chunk, low_bit(block))
        for chunk in range(chunks):
            yield last + chunk * pace
            finish(chunk, summed(0, chunk))
        for copy in sent.values():
            copy.wait_send()


def norm_back_parts(value, gain, gradient):
    xh, rate = norm_parts(value)
    mg = gradient * gain
    back = rate * (
        mg - jnp.mean(mg, axis=-1, keepdims=True) - xh * jnp.mean(mg * xh, axis=-1, keepdims=True)
    )
    return back, jnp.sum(gradient * xh, axis=0, keepdims=True), jnp.sum(gradient, axis=0, keepdims=True)


def stream_flow(
    value=None,
    gain=None,
    shift=None,
    terms=None,
    above=None,
    rs=1,
    ag=1,
    keep=True,
    late=None,
    everyone=(),
    clock=(5, 30, 6, 60),
    gather_clock=(30, 6),
):
    if value is None:
        tokens, model = terms.shape[0] // rs, terms.shape[1]
    else:
        tokens, model = value.shape
    ag_bits = bits_of(ag)
    chunks = 4 if tokens % 64 == 0 else 1
    part = tokens // chunks
    flow = Flow([(TENSOR, bit) for bit in bits_of(max(rs, ag))] + list(everyone))
    if value is not None:
        value_key = flow.take(value, VMEM)
        gain_key = flow.take(gain[None], VMEM)
    if shift is not None:
        shift_key = flow.take(shift[None], VMEM)
    if above is not None:
        above_key = flow.take(above, VMEM)
        gain_sum = flow.give((1, model), F32, VMEM)
        shift_sum = flow.give((1, model), F32, VMEM)
    if rs > 1:
        terms_key = flow.take(terms)
        total_of = Sum(flow, rs, chunks, tokens, model)
    if keep:
        stream_key = flow.give((tokens, model), F32, VMEM)
    result_key = flow.give((ag * tokens, model), BF16, HBM if ag > 1 else VMEM)
    if ag > 1:
        own_key = flow.vmem(tokens, model)
        keep_sem = flow.sems(chunks)
        ag_send = flow.sems(ag, chunks)
        ag_recv = flow.sems(ag, chunks)
    if late is not None:
        late_key = flow.take(late, VMEM)
        all_key = flow.give((8, model), F32, VMEM)
        totals_key = flow.vmem(len(everyone) + 1, 8, model, dtype=F32)
        others_key = flow.vmem(len(everyone), 8, model, dtype=F32)
        totals_send = flow.sems(len(everyone))
        totals_recv = flow.sems(len(everyone))

    def rows(chunk):
        return pl.ds(chunk * part, part)

    def steps(r):
        t = lax.axis_index(TENSOR)

        def at(block, group, chunk):
            start = (peer(t, block) % group) * tokens + chunk * part
            return pl.ds(pl.multiple_of(start, 16), part)

        sent, keeps = {}, []

        def send(src, dst, block, chunk, bit):
            sent[block, chunk] = remote(
                src,
                dst,
                r[ag_send].at[block, chunk],
                r[ag_recv].at[block, chunk],
                TENSOR,
                partner(t, bit),
            )

        def finish(chunk, total):
            here = rows(chunk)
            if value is None:
                r[result_key][here, :] = total.astype(BF16)
                return
            stream = r[value_key][here, :].astype(F32)
            if above is None:
                if total is not None:
                    stream = stream + total
                    r[stream_key][here, :] = stream
                xh, unused = norm_parts(stream)
                result = (xh * r[gain_key][...] + r[shift_key][...]).astype(BF16)
            else:
                back, gains, shifts = norm_back_parts(stream, r[gain_key][...], total)
                if chunk == 0:
                    r[gain_sum][...] = gains
                    r[shift_sum][...] = shifts
                else:
                    r[gain_sum][...] += gains
                    r[shift_sum][...] += shifts
                gradient = r[above_key][here, :].astype(F32) + back
                if keep:
                    r[stream_key][here, :] = gradient
                result = gradient.astype(BF16)
            if ag == 1:
                r[result_key][here, :] = result
                return
            r[own_key][here, :] = result
            place = r[result_key].at[at(0, ag, chunk)]
            keeps.append(local_copy(r[own_key].at[here], place, r[keep_sem].at[chunk]))
            for bit in reversed(ag_bits):
                send(r[own_key].at[here], place, bit, chunk, bit)

        if rs > 1:
            yield from total_of.steps(
                r,
                lambda block, chunk: r[terms_key].at[at(block, rs, chunk)],
                rows,
                finish,
                clock,
            )
        else:
            for chunk in range(chunks):
                finish(chunk, None)
        if late is not None:
            count = late.shape[0]
            totals, others = r[totals_key], r[others_key]
            totals[0, :count] = r[late_key][...]
            totals[0, count : count + 1] = r[gain_sum][...]
            totals[0, count + 1 : count + 2] = r[shift_sum][...]
            totals[0, count + 2 :] = jnp.zeros_like(totals[0, count + 2 :])
            for i, (axis, bit) in enumerate(everyone):
                copy = remote(
                    totals.at[i],
                    others.at[i],
                    r[totals_send].at[i],
                    r[totals_recv].at[i],
                    axis,
                    partner(lax.axis_index(axis), bit),
                )
                yield clock[-1] + 40 + 15 * i
                copy.wait()
                totals[i + 1] = totals[i] + others[i]
            r[all_key][...] = totals[len(everyone)]
        first, pace = gather_clock
        for i, block in enumerate(sorted(range(2, ag, 2), key=lambda b: (level_of(b), low_bit(b)))):
            for chunk in range(chunks):
                yield first + (i * chunks + chunk) * pace
                sent[block, chunk].wait_recv()
                for bit in reversed(ag_bits):
                    if bit < low_bit(block):
                        place = r[result_key].at[at(block, ag, chunk)]
                        send(place, place, block + bit, chunk, bit)
        for (block, chunk), copy in sent.items():
            copy.wait_send()
            if block % 2:
                copy.wait_recv()
        for copy in keeps:
            copy.wait()

    flow.steps = steps
    return flow


def spread_on(side, block, bit):
    if block == 0:
        return True
    return bit < low_bit(block) if side == 0 else bit > high_bit(block)


def fetch_flow(weights, half, n_dp, window=3, clock=(8, 6.5)):
    dp_bits = bits_of(n_dp)
    units = [
        (which, plane, side)
        for which, (by_rows, weight) in enumerate(weights)
        for plane in range(weight.shape[0])
        for side in range(2)
    ]
    flow = Flow([(TENSOR, half)] + [(DP, bit) for bit in dp_bits])
    sources, targets, owns = [], [], []
    for by_rows, weight in weights:
        planes, high, wide = weight.shape
        sources.append(flow.take(weight))
        both = (planes, 2 * high, wide) if by_rows else (planes, high, 2 * wide)
        targets.append(flow.give(both, BF16))
        owns.append(flow.vmem(*weight.shape))
    sends = flow.sems(len(units), n_dp)
    recvs = flow.sems(len(units), n_dp)
    takes = flow.sems(len(weights))
    keep_sems = flow.sems(len(weights))

    def steps(r):
        t = lax.axis_index(TENSOR)
        d = lax.axis_index(DP)
        copies, keeps = {}, []

        def places(unit, block):
            which, plane, side = unit
            by_rows, weight = weights[which]
            source, target = r[sources[which]], r[targets[which]]
            high, wide = weight.shape[1:]
            size = (wide if by_rows else high) // n_dp // 2
            start = (peer(d, block) * 2 + side) * size
            if by_rows:
                columns = pl.ds(pl.multiple_of(start, 128), size)
                return source.at[plane, :, columns], target.at[plane, pl.ds(high, high), columns]
            rows = pl.ds(pl.multiple_of(start, 16), size)
            return source.at[plane, rows], target.at[plane, rows, pl.ds(wide, wide)]

        def send(src, dst, unit, block, axis, index):
            copies[unit, block] = remote(
                src, dst, r[sends].at[unit, block], r[recvs].at[unit, block], axis, index
            )

        def begin(unit):
            if unit < len(units):
                src, dst = places(units[unit], 0)
                send(src, dst, unit, 0, TENSOR, partner(t, half))

        def forward(unit, block):
            copies[unit, block].wait_recv()
            place = places(units[unit], block)[1]
            for bit in dp_bits:
                if spread_on(units[unit][2], block, bit):
                    send(place, place, unit, block + bit, DP, partner(d, bit))

        for unit in range(window):
            begin(unit)
        for which in range(len(weights)):
            keeps.append(local_copy(r[sources[which]], r[owns[which]], r[takes].at[which]))
        yield clock[0]
        for which, (by_rows, weight) in enumerate(weights):
            high, wide = weight.shape[1:]
            target = r[targets[which]]
            target = target.at[:, pl.ds(0, high)] if by_rows else target.at[:, :, pl.ds(0, wide)]
            keeps[which].wait()
            keeps[which] = local_copy(r[owns[which]], target, r[keep_sems].at[which])
        for step in range(len(units) + len(dp_bits) - 1):
            if step < len(units):
                forward(step, 0)
                begin(step + window)
            for level in range(1, len(dp_bits)):
                if 0 <= step - level < len(units):
                    for block in range(1, n_dp):
                        if level_of(block) == level:
                            forward(step - level, block)
            yield clock[0] + (step + 1) * clock[1]
        for unit in range(len(units)):
            copies[unit, n_dp - 1].wait_recv()
        for copy in copies.values():
            copy.wait_send()
        for copy in keeps:
            copy.wait()

    flow.steps = steps
    return flow


def text_flow(text, half, n, clock=(20, 12)):
    high, wide = text.shape[0] // (n // half), text.shape[1]
    flow = Flow([(TENSOR, bit) for bit in bits_of(n)])
    text_key = flow.take(text)
    result_key = flow.give((high, wide * n), BF16)
    own_key = flow.vmem(high, wide)
    sends, recvs, keeps = flow.sems(n), flow.sems(n), flow.sems(2)

    def steps(r):
        t = lax.axis_index(TENSOR)
        row = t // half
        copies = {}

        def rows(which):
            return r[text_key].at[pl.ds(pl.multiple_of(which * high, 16), high)]

        def columns(block):
            return r[result_key].at[:, pl.ds(pl.multiple_of(peer(t, block) * wide, 128), wide)]

        def send(src, dst, block, bit):
            copies[block] = remote(
                src, dst, r[sends].at[block], r[recvs].at[block], TENSOR, partner(t, bit)
            )

        for bit in reversed(bits_of(n)):
            send(rows(1 - row if bit == half else row), columns(0), bit, bit)
        keep = local_copy(rows(row), r[own_key], r[keeps].at[0])
        yield clock[0]
        keep.wait()
        keep = local_copy(r[own_key], columns(0), r[keeps].at[1])
        for i, block in enumerate(sorted(range(1, n), key=lambda b: (level_of(b), low_bit(b)))):
            copies[block].wait_recv()
            for bit in reversed(bits_of(n)):
                if bit < low_bit(block):
                    send(columns(block), columns(block), block + bit, bit)
            yield clock[0] + i * clock[1]
        for copy in copies.values():
            copy.wait_send()
        keep.wait()

    flow.steps = steps
    return flow


def text_back_flow(terms, half, n, clocks=((8, 30, 6, 30), (9, 30, 6, 35), 45)):
    high, wide = terms.shape[0], terms.shape[1] // n
    flow = Flow([(TENSOR, bit) for bit in bits_of(n)])
    terms_key = flow.take(terms)
    result_key = flow.give((high * (n // half), wide), BF16)
    sums = [Sum(flow, half, 1, high, wide) for unused in range(2)]
    owns = [flow.vmem(high, wide) for unused in range(2)]
    sems = flow.sems(3)

    def steps(r):
        t = lax.axis_index(TENSOR)
        row = t // half
        last = []

        def view(far):
            def place(block, chunk):
                column = peer(t, block + far) * wide
                return r[terms_key].at[:, pl.ds(pl.multiple_of(column, 128), wide)]

            return place

        def target():
            return r[result_key].at[pl.ds(pl.multiple_of(row * high, 16), high)]

        def finish_far(chunk, total):
            r[owns[0]][...] = total.astype(BF16)
            last.append(
                remote(
                    r[owns[0]],
                    target(),
                    r[sems].at[0],
                    r[sems].at[1],
                    TENSOR,
                    partner(t, half),
                )
            )

        def finish_near(chunk, total):
            r[owns[1]][...] = total.astype(BF16)
            last.append(local_copy(r[owns[1]], target(), r[sems].at[2]))

        def rows(chunk):
            return pl.ds(0, high)

        parts = [
            [0, sums[0].steps(r, view(half), rows, finish_far, clocks[0])],
            [0, sums[1].steps(r, view(0), rows, finish_near, clocks[1])],
        ]
        while parts:
            entry = min(parts, key=lambda e: e[0])
            if entry[0]:
                yield entry[0]
            moment = next(entry[1], None)
            if moment is None:
                parts.remove(entry)
            else:
                entry[0] = moment
        yield clocks[2]
        for copy in last:
            copy.wait()

    flow.steps = steps
    return flow


def grads_flow(grads, n_dp, half=0, summing=True, window=4, clock=(10, 20)):
    high, whole = grads[0].shape[1:]
    high = high if summing else high * n_dp
    wide = whole // 2 if half else whole
    size = high // n_dp // 2
    dp_bits = bits_of(n_dp)
    units = [
        (which, plane, side)
        for which, grad in enumerate(grads)
        for plane in range(grad.shape[0])
        for side in range(2)
    ]
    count = len(units)
    depth = len(dp_bits)
    slots = n_dp // 2 if summing else 1
    flow = Flow([(DP, bit) for bit in dp_bits] + ([(TENSOR, half)] if half else []))
    sources = [flow.take(grad) for grad in grads]
    targets = [flow.give((grad.shape[0], high, wide), BF16) for grad in grads]
    held = flow.vmem(count, slots, size, whole if summing else wide)
    load_sems = flow.sems(count, slots)
    if summing:
        came = flow.vmem(count, n_dp - 1, size, whole)
        sum_send, sum_recv = flow.sems(count, n_dp), flow.sems(count, n_dp)
    if half:
        given = flow.vmem(count, size, wide)
        mid_send, mid_recv = flow.sems(count), flow.sems(count)
        if summing:
            mine = flow.vmem(count, size, wide, dtype=F32)
            theirs = flow.vmem(count, size, wide)
    final = flow.vmem(count, size, wide)
    ag_send, ag_recv = flow.sems(count, n_dp), flow.sems(count, n_dp)
    keep_sems = flow.sems(count)

    def order(side):
        return dp_bits if side == 0 else tuple(reversed(dp_bits))

    def stage(side, block):
        return min(i for i, bit in enumerate(order(side)) if block & bit)

    def slot(side, block):
        return [b for b in range(n_dp) if b == 0 or stage(side, b) > 0].index(block)

    def steps(r):
        d = lax.axis_index(DP)
        sums, loads, mids, spreads, keeps = {}, {}, {}, {}, {}

        def region(keys, unit, block, piece=False):
            which, plane, side = units[unit]
            start = side * size if piece else (peer(d, block) * 2 + side) * size
            return r[keys[which]].at[plane, pl.ds(pl.multiple_of(start, 16), size)]

        def swap(src, unit):
            mids[unit] = remote(
                src,
                r[given].at[unit],
                r[mid_send].at[unit],
                r[mid_recv].at[unit],
                TENSOR,
                partner(lax.axis_index(TENSOR), half),
            )

        def send(src, unit, block):
            side = units[unit][2]
            sums[unit, block] = remote(
                src,
                r[came].at[unit, block - 1],
                r[sum_send].at[unit, block],
                r[sum_recv].at[unit, block],
                DP,
                partner(d, order(side)[stage(side, block)]),
            )

        def summed(unit, block):
            side = units[unit][2]
            loads[unit, block].wait()
            total = r[held][unit, slot(side, block)].astype(F32)
            for i, bit in enumerate(order(side)):
                if summing and (block == 0 or i < stage(side, block)):
                    sums[unit, block + bit].wait_recv()
                    total = total + r[came][unit, block + bit - 1].astype(F32)
            return total

        def begin(unit):
            if unit >= count:
                return
            side = units[unit][2]
            if not summing:
                source = region(sources, unit, 0, True)
                swap(source.at[:, pl.ds(wide, wide)], unit)
                loads[unit, 0] = local_copy(
                    source.at[:, pl.ds(0, wide)], r[held].at[unit, 0], r[load_sems].at[unit, 0]
                )
                return
            for block in range(n_dp):
                source = region(sources, unit, block)
                if block and stage(side, block) == 0:
                    send(source, unit, block)
                else:
                    place = slot(side, block)
                    loads[unit, block] = local_copy(
                        source, r[held].at[unit, place], r[load_sems].at[unit, place]
                    )

        def middle(unit, level):
            side = units[unit][2]
            for block in range(1, n_dp):
                if stage(side, block) == level:
                    r[held][unit, slot(side, block)] = summed(unit, block).astype(BF16)
                    send(r[held].at[unit, slot(side, block)], unit, block)

        def cross(unit):
            if half and summing:
                total = summed(unit, 0)
                r[mine][unit] = total[:, :wide]
                r[theirs][unit] = total[:, wide:].astype(BF16)
                swap(r[theirs].at[unit], unit)

        def spread(unit, block, src, dst):
            for bit in dp_bits:
                if spread_on(units[unit][2], block, bit):
                    spreads[unit, block + bit] = remote(
                        src,
                        dst,
                        r[ag_send].at[unit, block + bit],
                        r[ag_recv].at[unit, block + bit],
                        DP,
                        partner(d, bit),
                    )

        def settle(unit):
            total = r[mine][unit] if half and summing else summed(unit, 0)
            if half:
                mids[unit].wait_recv()
                total = total + r[given][unit].astype(F32)
            r[final][unit] = total.astype(BF16)
            place = region(targets, unit, 0)
            keeps[unit] = local_copy(r[final].at[unit], place, r[keep_sems].at[unit])
            spread(unit, 0, r[final].at[unit], place)

        def onward(unit, level):
            for block in range(1, n_dp):
                if level_of(block) == level:
                    spreads[unit, block].wait_recv()
                    place = region(targets, unit, block)
                    spread(unit, block, place, place)

        for unit in range(window):
            begin(unit)
        first = depth if summing else 0
        for step in range(count + first + depth):
            yield clock[0] + step * clock[1]

            def turn(lag, action, *more):
                if 0 <= step - lag < count:
                    action(step - lag, *more)

            for level in range(depth - 1, 0, -1):
                turn(first + level, onward, level)
            turn(first, settle)
            turn(max(first - 1, 0), cross)
            if summing:
                for level in range(depth - 1, 0, -1):
                    turn(level - 1, middle, level)
            begin(step + window)
        for unit in range(count):
            spreads[unit, n_dp - 1].wait_recv()
        for copy in [*sums.values(), *mids.values(), *spreads.values()]:
            copy.wait_send()
        for copy in keeps.values():
            copy.wait()

    flow.steps = steps
    return flow


def pass_flow(value):
    flow = Flow([])
    value_key = flow.take(value)
    result_key = flow.give(value.shape, value.dtype)
    held = flow.vmem(*value.shape)
    sems = flow.sems(2)

    def steps(r):
        copy = local_copy(r[value_key], r[held], r[sems].at[0])
        yield 8
        copy.wait()
        copy = local_copy(r[held], r[result_key], r[sems].at[1])
        yield 30
        copy.wait()

    flow.steps = steps
    return flow


def nothing(*refs):
    pass


def after(value, *before):
    return pl.pallas_call(
        nothing,
        in_specs=[HBM] * (1 + len(before)),
        out_specs=HBM,
        out_shape=jax.ShapeDtypeStruct(value.shape, value.dtype),
        input_output_aliases={0: 0},
    )(value, *before)


def local(
    image,
    text,
    cotangent,
    norm_gains,
    norm_shifts,
    w_self,
    w_self_out,
    w_cross_q,
    w_cross_kv,
    w_cross_out,
    w_text,
    w_up,
    w_down,
    segment_ids,
    caption_lengths,
):
    rows_here = segment_ids.shape[0]
    n_tensor = lax.axis_size(TENSOR)
    n_dp = lax.axis_size(DP)
    half = n_tensor // rows_here
    row = lax.axis_index(TENSOR) // half
    width = w_self.shape[2]
    slots = IMGS * CAP

    seg = lax.dynamic_index_in_dim(segment_ids, row, 0, keepdims=False)
    seg_col = seg[:, None]
    seg_row = seg[None, :]
    lengths = lax.dynamic_index_in_dim(caption_lengths.reshape(rows_here, IMGS), row, 0, keepdims=False)
    slot = jnp.arange(slots, dtype=jnp.int32)
    live = (slot % CAP) < jnp.repeat(lengths, CAP)
    slot_row = jnp.where(live, slot // CAP, -1)[None, :]

    (w_self2, w_self_out2), (n1,), (later,) = run_flows(
        0,
        "start",
        60,
        fetch_flow(((False, w_self), (True, w_self_out[None])), half, n_dp),
        stream_flow(
            image, norm_gains[0], norm_shifts[0], ag=half, keep=False, gather_clock=(12, 11)
        ),
        pass_flow(cotangent),
    )
    w_self_out2 = w_self_out2[0]
    triple = planes_of(n1, w_self2)
    o1 = attend(seg_col, seg_row, (triple, 0), (triple, 1), (triple, 2))
    p1 = dot(o1, w_self_out2).astype(BF16)
    e3 = lax.all_gather(later, TENSOR, axis=0, tiled=True)
    text_columns = dot(text, w_text).astype(BF16)
    (x1, n2), (w_kv2, w_cross_q2, w_cross_out2), (projected,) = run_flows(
        1,
        "self_sum",
        100,
        stream_flow(
            image,
            norm_gains[1],
            norm_shifts[1],
            terms=p1,
            rs=half,
            ag=half,
            clock=(5, 0, 10, 18),
            gather_clock=(60, 10),
        ),
        fetch_flow(
            ((False, w_cross_kv), (False, w_cross_q[None]), (True, w_cross_out[None])),
            half,
            n_dp,
            clock=(20, 8),
        ),
        text_flow(text_columns, half, n_tensor),
    )
    w_cross_q2, w_cross_out2 = w_cross_q2[0], w_cross_out2[0]

    pair = planes_of(projected, w_kv2)
    q2 = dot(n2, w_cross_q2).astype(BF16)
    o2 = attend(seg_col, slot_row, (q2, None), (pair, 0), (pair, 1))
    p2 = dot(o2, w_cross_out2).astype(BF16)
    ((x2, n3),) = run_flows(
        2,
        "cross_sum",
        100,
        stream_flow(x1, norm_gains[2], norm_shifts[2], terms=p2, rs=half, ag=n_tensor),
    )

    h = dot(n3, w_up)
    act, slope = gelu_parts(h)
    act = act.astype(BF16)
    slope = slope.astype(BF16)
    down_grad = dot_t(act, e3).astype(BF16)
    dh = (dot_r(e3, w_down) * slope.astype(F32)).astype(BF16)
    up_grad = dot_t(n3, dh).astype(BF16)
    sums = lax.psum((down_grad, up_grad), DP)
    p3 = after(dot_r(dh, w_up).astype(BF16), down_grad, up_grad)
    ((gain_two, shift_two, g2, e2),) = run_flows(
        3,
        "up_sum",
        100,
        stream_flow(
            x2, norm_gains[2], terms=p3, above=cotangent, rs=n_tensor, ag=half, clock=(8, 30, 6, 60)
        ),
    )

    do2 = dot_r(e2, w_cross_out2).astype(BF16)
    dq2, dk2, dv2 = attend_back(seg_col, slot_row, (q2, None), (pair, 0), (pair, 1), do2)
    p4 = dot_r(dq2, w_cross_q2).astype(BF16)
    pair_back = jnp.stack([dk2, dv2])
    cross = jnp.concatenate(
        [
            dot_t(n2, dq2).astype(BF16)[None],
            planes_grad(projected, pair_back),
            dot_t(e2, o2).astype(BF16)[None],
        ]
    )
    cross_part = lax.psum_scatter(cross, DP, scatter_dimension=1, tiled=True)
    dproj = planes_back(pair_back, w_kv2)
    (gain_one, shift_one, g1, e1), (dproj,) = run_flows(
        4,
        "query_sum",
        60,
        stream_flow(
            x1,
            norm_gains[1],
            terms=after(p4, cross),
            above=g2,
            rs=half,
            ag=half,
            clock=(5, 0, 6, 15),
            gather_clock=(37, 6),
        ),
        text_back_flow(dproj, half, n_tensor),
    )

    p6 = dot(after(act, e1), w_down).astype(BF16)
    down_sum = lax.psum_scatter(p6, TENSOR, scatter_dimension=0, tiled=True)
    image_out = (x2 + down_sum.astype(F32)).astype(BF16)

    do1 = dot_r(e1, w_self_out2).astype(BF16)
    dq1, dk1, dv1 = attend_back(seg_col, seg_row, (triple, 0), (triple, 1), (triple, 2), do1)
    triple_back = jnp.stack([dq1, dk1, dv1])
    own = planes_grad(n1, triple_back)
    own_out = dot_t(e1, o1).astype(BF16)[None]
    p5 = planes_back(triple_back, w_self2)
    text_w_part = dot_t(text, dproj).astype(BF16)
    p7 = dot_r(dproj, w_text).astype(BF16)
    everyone = [(TENSOR, bit) for bit in bits_of(n_tensor)] + [(DP, bit) for bit in bits_of(n_dp)]
    late = jnp.concatenate([gain_one, shift_one, gain_two, shift_two])
    (own, own_out), (unused, unused, image_grad, all_sums), (text_grad,), (cross,), (text_w,) = run_flows(
        5,
        "end",
        180,
        grads_flow((own, own_out), n_dp, half, clock=(20, 20)),
        stream_flow(
            image,
            norm_gains[0],
            terms=p5,
            above=g1,
            rs=half,
            keep=False,
            late=late,
            everyone=everyone,
            clock=(6, 0, 8, 50),
        ),
        stream_flow(terms=p7, rs=n_tensor, keep=False, clock=(7, 45, 11, 110)),
        grads_flow((cross_part,), n_dp, half, summing=False, clock=(15, 12)),
        grads_flow((text_w_part.reshape(4, -1, width),), n_dp, clock=(10, 16)),
    )
    self_grad = own.astype(F32)
    self_out_grad = own_out[0].astype(F32).T
    cross = cross.astype(F32)
    cross_q_grad = cross[0]
    cross_kv_grad = cross[1:3]
    cross_out_grad = cross[3].T
    text_w_grad = text_w.astype(F32).reshape(-1, width)
    down_grad, up_grad = [value.astype(F32) for value in sums]
    gain_grad = jnp.stack([all_sums[4], all_sums[0], all_sums[2]])
    shift_grad = jnp.stack([all_sums[5], all_sums[1], all_sums[3]])
    return (
        image_out,
        image_grad,
        text_grad,
        gain_grad,
        shift_grad,
        self_grad,
        self_out_grad,
        cross_q_grad,
        cross_kv_grad,
        cross_out_grad,
        text_w_grad,
        up_grad,
        down_grad,
    )


def solution(mesh):
    tokens = P((DP, TENSOR), None)
    columns = P(None, TENSOR)
    planes = P(None, None, TENSOR)
    rows = P(TENSOR, None)
    return jax.shard_map(
        local,
        mesh=mesh,
        in_specs=(
            tokens,
            P(DP, None),
            tokens,
            P(),
            P(),
            planes,
            rows,
            columns,
            planes,
            rows,
            columns,
            columns,
            rows,
            P(DP, None),
            P(DP),
        ),
        out_specs=(
            tokens,
            tokens,
            tokens,
            P(),
            P(),
            planes,
            rows,
            columns,
            planes,
            rows,
            columns,
            columns,
            rows,
        ),
        check_vma=False,
    )
```

time: 1870 us -> 1050 us (0.56)
  waiting for transfers between devices: 1230 us -> 0.8 us
  Pallas kernels: 0 us -> 791 us
  matrix products: 388 us -> 177 us
  local copies, waits for them, and re-layouts: 103 us -> 24.5 us
  other arithmetic: 75.2 us -> 33.7 us
  blocking collectives: 40.4 us -> 0 us
    pallas_call x0 -> x13, Pallas kernels: none -> 791 us  [the longest x6 737 us: run_flows(): pl.pallas_call(functools.partial(flows_kernel, flows), in_specs=[entry[1]...]
    reduce_scatter x8 -> x2, waiting for transfers between devices: 478 us -> 0.01 us  [the longest x1 0.01 us: local(): cross_part = lax.psum_scatter(cross, DP, scatter_dimension=1, tiled=True)]
    all_gather x7 -> x1, waiting for transfers between devices: 453 us -> 0.01 us  [local(): e3 = lax.all_gather(later, TENSOR, axis=0, tiled=True)]
    psum x1, waiting for transfers between devices: 302 us -> 0.02 us  [local(): sums = lax.psum((down_grad, up_grad), DP)]
    dot_general x38 -> x24, matrix products: 388 us -> 177 us  [the longest x6 52.2 us: dot_r(): lax.dot_general(left, right, (((1,), (1,)), ((), ())), preferred_element_...]
    psum x1 -> x0, blocking collectives: 40.4 us -> none  [local(): gain_grad, shift_grad = lax.psum((gain_grad, shift_grad), ('dp', 'tensor'))]
    another operation x17 -> x0, local copies, waits for them, and re-layouts: 37.1 us -> none  [the longest x8 19.3 us: split_heads(): return flat.reshape(row_count, -1, local_heads, HD)]
    reduce_sum x14 -> x0, other arithmetic: 32.4 us -> none  [the longest x5 13.7 us: layer_norm(): return centered * lax.rsqrt(spread + epsilon) * gain + shift]
  transfers between devices with their start and end apart: 16 -> 4, of which waited for: 14 -> 0; matrix products, arithmetic and copies ran while one was open for 20% -> 16% of each run, Pallas kernels for 0% -> 69%
where the time goes in v1:
time: 1050 us; the launch traced here: 1040 us
  Pallas kernels  791 us (75%)
  matrix products  177 us (17%)
  other arithmetic  33.7 us (3%)
  local copies, waits for them, and re-layouts  24.5 us (2%)
  between operations  14.6 us (1%)
    pallas_call x6, Pallas kernels, run_flows(): pl.pallas_call(functools.partial(flows_kernel, flows), in_specs=[entry[1]...  737 us
    dot_general x6, matrix products, dot_r(): lax.dot_general(left, right, (((1,), (1,)), ((), ())), preferred_element_...  52.2 us
    dot_general x6, matrix products, dot(): return jnp.dot(left, right, preferred_element_type=F32)  47.8 us
    dot_general x6, matrix products, dot_t(): lax.dot_general(left, right, (((0,), (0,)), ((), ())), preferred_element_...  38.4 us
    pallas_call x2, Pallas kernels, attend_back(): pl.pallas_call(functools.partial(attend_back_kernel, 256), grid=(heads,),...  33.5 us
  transfers between devices with their start and end apart: 4, of which 0 were waited for; matrix products, arithmetic and copies ran while one was open for 16% of the time, Pallas kernels for 69%

profile of v1, /device:TPU:0, one launch (start us, length us, event | category | flops | bytes accessed | tf_op | source)
XLA Modules:
  0.0 1042.1 jit_solution(3982147360836255333)
XLA Ops:
  7.2 0.0 all-gather.2.cloned.1.call-start
  7.3 1.6 fusion.48
  8.9 71.3 %start.1 = (bf16[3,2048,512]{2,1,0:T(8,128)(2,1)}, bf16[1,512,2048]{2,1,0:T(8,128)(2,1)}, bf16[1024,2048]{1,0:T(8,128)(2,1)}, bf16[256,2048]{1,0:T(8,128)(2,1)}) custom-call(bf16[3,2048,256]{2,1,0:T(8,128)(2,1)} %refs_0_.2, bf16[1,256,2048]{2,1,0:T(8,128)(2,1)} %bitcast.134, bf16[256,2048]{1,0:T(8,128)(2,1)} %refs_2_.5, ...), custom_call_target="tpu_custom_call" | custom-call | bytes 198000000 | tf_op jit(solution)/shard_map/start/pallas_call | solution.py:295
  80.2 0.0 all-gather.2.cloned.1.call-update
  80.2 0.1 reshape.106
  80.3 0.2 copy.44.qid_ref
  80.6 10.1 convert_bitcast_fusion.2.q_ref.k_ref.v_ref
  90.7 11.7 %attend.2 = bf16[1024,512]{1,0:T(8,128)(2,1)S(1)} custom-call(s32[1024,1]{1,0:T(8,128)S(1)} %copy.44.qid_ref, s32[1,1024]{1,0:T(1,128)S(1)} %constant_dynamic-slice_fusion.kid_ref, bf16[3,1024,512]{2,1,0:T(8,128)(2,1)S(1)} %convert_bitcast_fusion.2.q_ref.k_ref.v_ref, bf16[3,1024,512]{2,1,0:T(8,128)(2,1)S(1)} %convert_bitcast_fusion.2.q_ref.k_ref.v_ref, ...), custom_call_target="tpu_custom_call" | custom-call | flops 2147483648 | bytes 4194304 | tf_op jit(solution)/shard_map/attend/pallas_call | solution.py:87
  102.5 4.4 convolution_convert_fusion.7.refs_3_
  106.9 3.1 convolution_convert_fusion.12.refs_7_
  110.0 135.4 %self_sum.1 = (f32[256,2048]{1,0:T(8,128)}, bf16[1024,2048]{1,0:T(8,128)(2,1)}, bf16[2,2048,512]{2,1,0:T(8,128)(2,1)}, bf16[1,2048,512]{2,1,0:T(8,128)(2,1)}, bf...) custom-call(bf16[256,2048]{1,0:T(8,128)(2,1)} %refs_2_.5, f32[1,2048]{1,0:T(1,128)} %get-tuple-element.126.refs_1_, ...), custom_call_target="tpu_custom_call" | custom-call | bytes 330000000 | tf_op jit(solution)/shard_map/self_sum/pallas_call | solution.py:295
  245.5 0.1 broadcast_in_dim.32
  245.6 5.3 fusion.31.q_ref
  251.0 2.3 fusion.40.k_ref.v_ref
  253.3 8.4 attend.3
  261.8 4.4 convolution_convert_fusion.6.refs_3_
  266.1 113.2 %cross_sum.1 = (f32[256,2048]{1,0:T(8,128)}, bf16[2048,2048]{1,0:T(8,128)(2,1)}) custom-call(f32[256,2048]{1,0:T(8,128)} %get-tuple-element.50.refs_0_, f32[1,2048]{1,0:T(1,128)} %get-tuple-element.127.refs_1_, f32[1,2048]{1,0:T(1,128)} %get-tuple-element.117.refs_2_, bf16[1024,2048]{1,0:T(8,128)(2,1)} %convolution_convert_fusion.6.refs_3_), custom_call_target="tpu_custom_call" | custom-call | bytes 330000000 | tf_op jit(solution)/shard_map/cross_sum/pallas_call | solution.py:295
  379.3 16.4 %multiply_convert_fusion.1 = (bf16[2048,1024]{1,0:T(8,128)(2,1)}, f32[2048,1024]{1,0:T(8,128)}) fusion(bf16[2048,2048]{1,0:T(8,128)(2,1)} %get-tuple-element.57, bf16[2048,1024]{1,0:T(8,128)(2,1)} %param.26), kind=kOutput, calls=%fused_computation.12 | convolution fusion | flops 8608808960 | bytes 25165824 | tf_op jit(solution)/shard_map/dot_general | solution.py:143
  395.8 19.4 %multiply_convert_fusion = bf16[2048,1024]{1,0:T(8,128)(2,1)} fusion(bf16[2048,2048]{1,0:T(8,128)(2,1)} %all-gather.2.cloned.1.call-done, bf16[1024,2048]{1,0:T(8,128)(2,1)} %param.27, f32[2048,1024]{1,0:T(8,128)} %get-tuple-element.124), kind=kOutput, calls=%fused_computation.11 | convolution fusion | flops 8633974784 | bytes 25165824 | tf_op jit(solution)/shard_map/dot_general | solution.py:151
  415.2 12.2 %convolution_convert_fusion.8.refs_2_ = bf16[2048,1024]{1,0:T(8,128)(2,1)} fusion(bf16[2048,2048]{1,0:T(8,128)(2,1)S(1)} %copy-done.29, bf16[2048,1024]{1,0:T(8,128)(2,1)} %multiply_convert_fusion), kind=kOutput, calls=%fused_computation.29 | convolution fusion | flops 8592031744 | bytes 16777216 | tf_op jit(solution)/shard_map/dot_general | solution.py:147
  427.4 13.7 %convolution_convert_fusion.2.refs_0_ = bf16[2048,2048]{1,0:T(8,128)(2,1)} fusion(bf16[2048,1024]{1,0:T(8,128)(2,1)} %multiply_convert_fusion, bf16[2048,1024]{1,0:T(8,128)(2,1)S(1)} %copy-done.30), kind=kOutput, calls=%fused_computation.16 | convolution fusion | flops 8594128896 | bytes 16777216 | tf_op jit(solution)/shard_map/dot_general | solution.py:151
  441.1 10.5 %convolution_convert_fusion.5.refs_1_ = bf16[1024,2048]{1,0:T(8,128)(2,1)} fusion(bf16[2048,1024]{1,0:T(8,128)(2,1)S(1)} %copy-done.16, bf16[2048,2048]{1,0:T(8,128)(2,1)S(1)} %bitcast.137), kind=kOutput, calls=%fused_computation.26 | convolution fusion | flops 8592031744 | bytes 16777216 | tf_op jit(solution)/shard_map/dot_general | solution.py:147
  451.6 0.7 all-reduce.3.cloned.1.call-update
  452.4 0.3 reduce-scatter.5.cloned.1.call-start
  452.6 102.2 %up_sum.1 = (f32[1,2048]{1,0:T(1,128)}, f32[1,2048]{1,0:T(1,128)}, f32[256,2048]{1,0:T(8,128)}, bf16[1024,2048]{1,0:T(8,128)(2,1)}) custom-call(f32[256,2048]{1,0:T(8,128)} %get-tuple-element.56.refs_0_, f32[1,2048]{1,0:T(1,128)} %get-tuple-element.127.refs_1_, bf16[256,2048]{1,0:T(8,128)(2,1)} %refs_2_.4, bf16[2048,2048]{1,0:T(8,128)(2,1)} %shard_map.246.refs_3_), custom_call_target="tpu_custom_call" | custom-call | bytes 330000000 | tf_op jit(solution)/shard_map/up_sum/pallas_call | solution.py:295
  554.9 4.9 fusion.37.do_ref
  559.8 13.3 %attend_back.2 = (bf16[1024,512]{1,0:T(8,128)(2,1)S(1)}, bf16[512,512]{1,0:T(8,128)(2,1)S(1)}, bf16[512,512]{1,0:T(8,128)(2,1)S(1)}) custom-call(s32[1024,1]{1,0:T(8,128)S(1)} %copy.44.qid_ref, s32[1,512]{1,0:T(1,128)S(1)} %compare_select_fusion.kid_ref, bf16[1024,512]{1,0:T(8,128)(2,1)S(1)} %copy-done.9, bf16[2,512,512]{2,1,0:T(8,128)(2,1)S(1)} %copy-done.3, ...), custom_call_target="tpu_custom_call" | custom-call | flops 2684354560 | bytes 5242880 | tf_op jit(solution)/shard_map/attend_back/pallas_call | solution.py:114
  573.2 2.4 convert_bitcast_fusion.1
  575.6 0.6 copy-done.34
  576.2 2.4 fusion.12
  578.7 2.5 fusion.11
  581.1 3.8 pad_maximum_fusion.refs_1_
  584.9 0.5 reduce-scatter.3.cloned.1.call-start
  585.5 6.3 convolution_convert_fusion.4.refs_0_
  591.8 6.2 bitcast_convert_fusion.1.refs_4_
  597.9 75.4 %query_sum.1 = (f32[1,2048]{1,0:T(1,128)}, f32[1,2048]{1,0:T(1,128)}, f32[256,2048]{1,0:T(8,128)}, bf16[1024,2048]{1,0:T(8,128)(2,1)}, bf16[1024,256]{1,0:T(8,128)(2,1)}) custom-call(f32[256,2048]{1,0:T(8,128)} %get-tuple-element.50.refs_0_, f32[1,2048]{1,0:T(1,128)} %get-tuple-element.126.refs_1_, f32[256,2048]{1,0:T(8,128)} %get-tuple-element.59.refs_2_, ...), custom_call_target="tpu_custom_call" | custom-call | bytes 198000000 | tf_op jit(solution)/shard_map/query_sum/pallas_call | solution.py:295
  673.3 14.3 %convolution_convert_fusion.1 = bf16[2048,2048]{1,0:T(8,128)(2,1)} fusion(bf16[2048,1024]{1,0:T(8,128)(2,1)} %shard_map.248, bf16[1024,2048]{1,0:T(8,128)(2,1)} %param.27), kind=kOutput, calls=%fused_computation.15 | convolution fusion | flops 8594128896 | bytes 16777216 | tf_op jit(solution)/shard_map/dot_general | solution.py:143
  687.6 1.0 copy-done.18
  688.6 7.1 fusion.7
  695.7 4.1 copy.54
  699.8 0.7 pad_maximum_fusion.7.refs_6_
  700.5 5.6 convolution_convert_fusion.refs_7_
  706.1 2.4 fusion.28.do_ref
  708.5 20.1 %attend_back.3 = (bf16[1024,512]{1,0:T(8,128)(2,1)S(1)}, bf16[1024,512]{1,0:T(8,128)(2,1)S(1)}, bf16[1024,512]{1,0:T(8,128)(2,1)S(1)}) custom-call(s32[1024,1]{1,0:T(8,128)S(1)} %copy.44.qid_ref, s32[1,1024]{1,0:T(1,128)S(1)} %copy-done.11, bf16[3,1024,512]{2,1,0:T(8,128)(2,1)} %copy-done.1, bf16[3,1024,512]{2,1,0:T(8,128)(2,1)} %copy-done.1, ...), custom_call_target="tpu_custom_call" | custom-call | flops 5368709120 | bytes 7340032 | tf_op jit(solution)/shard_map/attend_back/pallas_call | solution.py:114
  728.7 3.8 fusion.13.refs_1_
  732.4 8.6 convert_bitcast_fusion.refs_0_
  741.1 8.6 bitcast_convert_fusion.refs_5_
  749.7 0.0 all-reduce.3.cloned.1.call-done
  749.7 6.9 convert_element_type.149
  756.6 4.4 convert_element_type.150
  761.1 239.9 %end.1 = (bf16[3,2048,256]{2,1,0:T(8,128)(2,1)}, bf16[1,2048,256]{2,1,0:T(8,128)(2,1)}, f32[1,2048]{1,0:T(1,128)}, f32[1,2048]{1,0:T(1,128)}, bf16[256,2048]{1,0...) custom-call(bf16[3,2048,512]{2,1,0:T(8,128)(2,1)} %convert_bitcast_f, ...), custom_call_target="tpu_custom_call" | custom-call | bytes 594000000 | tf_op jit(solution)/shard_map/end/pallas_call | solution.py:295
  1001.0 4.2 slice.64
  1005.2 4.1 convert_element_type.148
  1009.3 1.5 convert_bitcast_fusion.3
  1010.8 2.9 copy.55
  1013.7 4.5 slice_bitcast_fusion
  1018.2 2.9 copy.56
  1021.1 5.3 convert_element_type.146
  1026.4 0.6 pad_maximum_fusion.9
  1027.0 0.6 pad_maximum_fusion.8
  1027.7 2.5 bitcast_convert_fusion.2
  1030.1 3.3 add_convert_fusion
  1033.4 1.0 copy.72
  1034.4 1.0 copy.73
  (111 shorter events, 0.3 us)
Async XLA Ops:
  7.2 99.7 %copy-start = (bf16[4096,256]{1,0:T(8,128)(2,1)S(1)}, bf16[4096,256]{1,0:T(8,128)(2,1)}, u32[]{:S(2)}) copy-start(bf16[4096,256]{1,0:T(8,128)(2,1)} %param.25) | copy-start | bytes 6291460
  7.2 73.0 %copy-start.41 = (s32[8]{0:T(128)S(1)}, s32[8]{0:T(128)}, u32[]{:S(2)}) copy-start(s32[8]{0:T(128)} %param.29) | copy-start | bytes 100
  7.2 73.1 %copy-start.24 = (s32[2,1024]{1,0:T(2,128)S(1)}, s32[2,1024]{1,0:T(2,128)}, u32[]{:S(2)}) copy-start(s32[2,1024]{1,0:T(2,128)} %param.28) | copy-start | bytes 24580
  7.2 388.5 %all-gather.2.cloned.1.call-start = ((), (), s32[]{:S(2)}) async-start(), calls=%async_computation.2 | async-start | bytes 9437184 | tf_op jit(solution)/shard_map/all_gather | solution.py:996
  80.6 10.1 copy-start.10
  90.7 11.8 %copy-start.1 = (bf16[3,1024,512]{2,1,0:T(8,128)(2,1)}, bf16[3,1024,512]{2,1,0:T(8,128)(2,1)S(1)}, u32[]{:S(2)}) copy-start(bf16[3,1024,512]{2,1,0:T(8,128)(2,1)S(1)} %convert_bitcast_fusion.2.q_ref.k_ref.v_ref) | copy-start | bytes 9437188
  90.7 11.8 %copy-start.35 = (bf16[1,512,2048]{2,1,0:T(8,128)(2,1)S(1)}, bf16[1,512,2048]{2,1,0:T(8,128)(2,1)}, u32[]{:S(2)}) copy-start(bf16[1,512,2048]{2,1,0:T(8,128)(2,1)} %get-tuple-element.49) | copy-start | bytes 6291460
  90.7 16.2 %slice-start = ((s8[8388608]{0:T(1024)(128)(4,1)}), s8[4194304]{0:T(1024)(128)(4,1)S(1)}, s32[]{:S(2)}) async-start(s8[8388608]{0:T(1024)(128)(4,1)} %bitcast.129), calls=%async_computation.6 | async-start | bytes 8388608
  102.5 4.4 copy-start.4
  102.5 4.4 slice-start.1
  245.6 5.4 copy-start.32
  245.6 5.4 copy-start.37
  250.9 2.4 copy-start.8
  253.3 12.8 %copy-start.2 = (bf16[2,512,512]{2,1,0:T(8,128)(2,1)}, bf16[2,512,512]{2,1,0:T(8,128)(2,1)S(1)}, u32[]{:S(2)}) copy-start(bf16[2,512,512]{2,1,0:T(8,128)(2,1)S(1)} %fusion.40.k_ref.v_ref) | copy-start | bytes 3145732
  253.3 8.4 copy-start.39
  261.7 4.4 copy-start.6
  395.8 19.4 %copy-start.29 = (bf16[2048,2048]{1,0:T(8,128)(2,1)S(1)}, bf16[2048,2048]{1,0:T(8,128)(2,1)}, u32[]{:S(2)}) copy-start(bf16[2048,2048]{1,0:T(8,128)(2,1)} %get-tuple-element.57) | copy-start | bytes 25165828
  415.2 12.2 %copy-start.30 = (bf16[2048,1024]{1,0:T(8,128)(2,1)S(1)}, bf16[2048,1024]{1,0:T(8,128)(2,1)}, u32[]{:S(2)}) copy-start(bf16[2048,1024]{1,0:T(8,128)(2,1)} %param.26) | copy-start | bytes 12582916
  415.2 25.9 %slice-start.2 = ((s8[8388608]{0:T(1024)(128)(4,1)}), s8[4194304]{0:T(1024)(128)(4,1)S(1)}, s32[]{:S(2)}) async-start(s8[8388608]{0:T(1024)(128)(4,1)} %bitcast.136), calls=%async_computation.8 | async-start | bytes 8388608
  427.4 13.7 %copy-start.16 = (bf16[2048,1024]{1,0:T(8,128)(2,1)S(1)}, bf16[2048,1024]{1,0:T(8,128)(2,1)}, u32[]{:S(2)}) copy-start(bf16[2048,1024]{1,0:T(8,128)(2,1)} %get-tuple-element.123.refs_0_) | copy-start | bytes 12582916
  427.4 13.7 %slice-start.3 = ((s8[8388608]{0:T(1024)(128)(4,1)}), s8[4194304]{0:T(1024)(128)(4,1)S(1)}, s32[]{:S(2)}) async-start(s8[8388608]{0:T(1024)(128)(4,1)} %bitcast.136), calls=%async_computation.9 | async-start | bytes 8388608
  451.6 298.1 %all-reduce.3.cloned.1.call-start = ((), (), s32[]{:S(2)}) async-start(), calls=%async_computation.5 | async-start | bytes 16777216 | tf_op jit(solution)/shard_map/psum | solution.py:1040
  452.4 308.7 %reduce-scatter.5.cloned.1.call-start = ((), (), s32[]{:S(2)}) async-start(), calls=%async_computation.4 | async-start | bytes 10485760 | tf_op jit(solution)/shard_map/reduce_scatter | solution.py:1062
  452.6 102.2 %copy-start.40 = (bf16[1,512,2048]{2,1,0:T(8,128)(2,1)S(1)}, bf16[1,512,2048]{2,1,0:T(8,128)(2,1)}, u32[]{:S(2)}) copy-start(bf16[1,512,2048]{2,1,0:T(8,128)(2,1)} %get-tuple-element.55) | copy-start | bytes 6291460
  554.9 4.9 copy-start.3
  554.9 4.9 copy-start.9
  559.8 13.4 %copy-start.38 = (bf16[512,2048]{1,0:T(8,128)(2,1)S(1)}, bf16[512,2048]{1,0:T(8,128)(2,1)}, u32[]{:S(2)}) copy-start(bf16[512,2048]{1,0:T(8,128)(2,1)} %get-tuple-element.54) | copy-start | bytes 6291460
  573.2 2.5 copy-start.12
  573.2 5.5 copy-start.13
  573.2 2.4 copy-start.7
  573.2 3.0 copy-start.34
  576.2 2.4 copy-start.33
  584.9 445.2 %reduce-scatter.3.cloned.1.call-start = ((), (), s32[]{:S(2)}) async-start(), calls=%async_computation.3 | async-start | bytes 9437184 | tf_op jit(solution)/shard_map/reduce_scatter | solution.py:1082
  687.6 1.0 copy-start.18
  695.7 4.1 copy-start.25
  695.7 4.1 copy-start.26
  695.7 4.1 copy-start.27
  695.7 4.1 copy-start.28
  700.5 5.6 copy-start.17
  700.5 5.6 copy-start.36
  706.1 2.4 copy-start.11
  708.5 20.2 %copy-start.5 = (bf16[1024,512]{1,0:T(8,128)(2,1)S(1)}, bf16[1024,512]{1,0:T(8,128)(2,1)}, u32[]{:S(2)}) copy-start(bf16[1024,512]{1,0:T(8,128)(2,1)} %copy-done.4) | copy-start | bytes 3145732
  728.6 3.8 copy-start.31
  728.7 12.4 %slice-start.4 = ((s8[6291456]{0:T(1024)(128)(4,1)}), s8[4194304]{0:T(1024)(128)(4,1)S(1)}, s32[]{:S(2)}) async-start(s8[6291456]{0:T(1024)(128)(4,1)} %bitcast.138), calls=%async_computation.10 | async-start | bytes 8388608
  732.4 8.6 slice-start.5
  749.7 6.9 copy-start.15
  1000.9 4.3 copy-start.14
  1005.2 4.1 copy-start.20
  1021.1 5.3 copy-start.23
  1021.1 6.6 copy-start.19
  1030.1 4.2 copy-start.21
  1030.1 3.3 copy-start.22
Sparse Core Ops, SparseCore 0:
  80.3 121.2 all-gather.1
  456.8 170.9 all-reduce.2
  631.2 87.1 reduce-scatter.4
  720.5 147.4 reduce-scatter.2

commit v2 on v1

--- a/solution.py
+++ b/solution.py
@@ -11,6 +11,7 @@
 IMGS = 4
 CAP = 128
 SCALE = HD ** (-0.5)
+LOG2E = 1.4426950408889634
 MIB = 1024 * 1024
 
 epsilon = 1e-05
@@ -23,12 +24,11 @@
 BF16 = jnp.bfloat16
 
 
-def shares_of(q, k, allowed):
+def raised_of(q, k, allowed):
     raw = lax.dot_general(q, k, (((1,), (1,)), ((), ())), preferred_element_type=F32)
-    scores = jnp.where(allowed, raw * SCALE, masked_value)
-    highest = jnp.max(scores, axis=-1, keepdims=True)
-    raised = jnp.exp(scores - highest)
-    return raised * (1.0 / jnp.sum(raised, axis=-1, keepdims=True))
+    scores = jnp.where(allowed, raw * (SCALE * LOG2E), masked_value)
+    raised = jnp.exp2(scores - jnp.max(scores, axis=-1, keepdims=True))
+    return raised, 1.0 / jnp.sum(raised, axis=-1, keepdims=True)
 
 
 def attend_kernel(step, qid_ref, kid_ref, q_ref, k_ref, v_ref, o_ref):
@@ -37,9 +37,9 @@
     kid = kid_ref[...]
     for start in range(0, q_ref.shape[0], step):
         rows = pl.ds(start, step)
-        shares = shares_of(q_ref[rows, :], k, qid_ref[rows, :] == kid)
-        mixed = jnp.dot(shares.astype(BF16), v, preferred_element_type=F32)
-        o_ref[rows, :] = mixed.astype(BF16)
+        raised, rate = raised_of(q_ref[rows, :], k, qid_ref[rows, :] == kid)
+        mixed = jnp.dot(raised.astype(BF16), v, preferred_element_type=F32)
+        o_ref[rows, :] = (mixed * rate).astype(BF16)
 
 
 def attend_back_kernel(step, qid_ref, kid_ref, q_ref, k_ref, v_ref, do_ref, dq_ref, dk_ref, dv_ref, dk_sum, dv_sum):
@@ -50,14 +50,15 @@
         rows = pl.ds(start, step)
         q = q_ref[rows, :]
         do = do_ref[rows, :]
-        shares = shares_of(q, k, qid_ref[rows, :] == kid)
+        raised, rate = raised_of(q, k, qid_ref[rows, :] == kid)
         dp = lax.dot_general(do, v, (((1,), (1,)), ((), ())), preferred_element_type=F32)
-        inner = jnp.sum(dp * shares, axis=-1, keepdims=True)
-        ds = (SCALE * (shares * (dp - inner))).astype(BF16)
+        inner = jnp.sum(dp * raised, axis=-1, keepdims=True) * rate
+        ds = (raised * ((dp - inner) * (rate * SCALE))).astype(BF16)
         dq_ref[rows, :] = jnp.dot(ds, k, preferred_element_type=F32).astype(BF16)
         dk = lax.dot_general(ds, q, (((0,), (0,)), ((), ())), preferred_element_type=F32)
+        shared = (do.astype(F32) * rate).astype(BF16)
         dv = lax.dot_general(
-            shares.astype(BF16), do, (((0,), (0,)), ((), ())), preferred_element_type=F32
+            raised.astype(BF16), shared, (((0,), (0,)), ((), ())), preferred_element_type=F32
         )
         if start == 0:
             dk_sum[...] = dk
@@ -149,6 +150,65 @@
 
 def dot_r(left, right):
     return lax.dot_general(left, right, (((1,), (1,)), ((), ())), preferred_element_type=F32)
+
+
+def rows_dot_kernel(count, *refs):
+    total = None
+    for left_ref, right_ref in zip(refs[:count], refs[count : 2 * count]):
+        term = lax.dot_general(
+            left_ref[...], right_ref[...], (((1,), (1,)), ((), ())), preferred_element_type=F32
+        )
+        total = term if total is None else total + term
+    refs[-1][...] = total.astype(BF16)
+
+
+def rows_dot(lefts, right, tile=512):
+    count = len(lefts)
+    high, deep = lefts[0].shape
+    wide = right.shape[1]
+    return pl.pallas_call(
+        functools.partial(rows_dot_kernel, count),
+        grid=(wide // tile,),
+        in_specs=[pl.BlockSpec((high, deep), lambda n: (0, 0))] * count
+        + [pl.BlockSpec((None, tile, deep), lambda n, c=c: (c, n, 0)) for c in range(count)],
+        out_specs=pl.BlockSpec((high, tile), lambda n: (0, n)),
+        out_shape=jax.ShapeDtypeStruct((high, wide), BF16),
+        compiler_params=pltpu.CompilerParams(vmem_limit_bytes=48 * MIB),
+        cost_estimate=pl.CostEstimate(
+            flops=2 * count * high * deep * wide,
+            bytes_accessed=2 * (count * deep * (high + wide) + high * wide),
+            transcendentals=0,
+        ),
+        name="rows_dot",
+    )(*lefts, *[right] * count)
+
+
+def columns_dot_kernel(left_ref, right_ref, out_ref):
+    out_ref[...] = lax.dot_general(
+        left_ref[...], right_ref[...], (((0,), (0,)), ((), ())), preferred_element_type=F32
+    ).astype(BF16)
+
+
+def columns_dot(left, right, tile=512):
+    deep, high = left.shape
+    wide = right.shape[1]
+    return pl.pallas_call(
+        columns_dot_kernel,
+        grid=(high // tile,),
+        in_specs=[
+            pl.BlockSpec((deep, tile), lambda n: (0, n)),
+            pl.BlockSpec((deep, wide), lambda n: (0, 0)),
+        ],
+        out_specs=pl.BlockSpec((tile, wide), lambda n: (n, 0)),
+        out_shape=jax.ShapeDtypeStruct((high, wide), BF16),
+        compiler_params=pltpu.CompilerParams(vmem_limit_bytes=48 * MIB),
+        cost_estimate=pl.CostEstimate(
+            flops=2 * deep * high * wide,
+            bytes_accessed=2 * (deep * (high + wide) + high * wide),
+            transcendentals=0,
+        ),
+        name="columns_dot",
+    )(left, right)
 
 
 def planes_of(left, right):
@@ -738,7 +798,7 @@
     return flow
 
 
-def grads_flow(grads, n_dp, half=0, summing=True, window=4, clock=(10, 20)):
+def grads_flow(grads, n_dp, outs, half=0, summing=True, window=4, clock=(10, 20), slack=1):
     high, whole = grads[0].shape[1:]
     high = high if summing else high * n_dp
     wide = whole // 2 if half else whole
@@ -755,8 +815,15 @@
     slots = n_dp // 2 if summing else 1
     flow = Flow([(DP, bit) for bit in dp_bits] + ([(TENSOR, half)] if half else []))
     sources = [flow.take(grad) for grad in grads]
-    targets = [flow.give((grad.shape[0], high, wide), BF16) for grad in grads]
-    held = flow.vmem(count, slots, size, whole if summing else wide)
+    targets = [flow.give((n, high, wide) if n else (wide, high), BF16) for n in outs]
+    target_of = [(i, plane) for i, n in enumerate(outs) for plane in range(max(n, 1))]
+    flat = [(grad, plane) for grad in range(len(grads)) for plane in range(grads[grad].shape[0])]
+    gathered = flow.vmem(len(flat), high, wide)
+    turned = [unit for unit in range(count) if not outs[target_of[flat.index(units[unit][:2])][0]]]
+    if turned:
+        staged = flow.vmem(len(turned), n_dp, wide, size)
+    if summing:
+        held = flow.vmem(count, slots, size, whole)
     load_sems = flow.sems(count, slots)
     if summing:
         came = flow.vmem(count, n_dp - 1, size, whole)
@@ -767,9 +834,8 @@
         if summing:
             mine = flow.vmem(count, size, wide, dtype=F32)
             theirs = flow.vmem(count, size, wide)
-    final = flow.vmem(count, size, wide)
     ag_send, ag_recv = flow.sems(count, n_dp), flow.sems(count, n_dp)
-    keep_sems = flow.sems(count)
+    keep_sems = flow.sems(count, n_dp)
 
     def order(side):
         return dp_bits if side == 0 else tuple(reversed(dp_bits))
@@ -782,12 +848,18 @@
 
     def steps(r):
         d = lax.axis_index(DP)
-        sums, loads, mids, spreads, keeps = {}, {}, {}, {}, {}
-
-        def region(keys, unit, block, piece=False):
+        sums, loads, mids, spreads, keeps = {}, {}, {}, {}, []
+
+        def rows_of(unit, block):
+            return pl.ds(pl.multiple_of((peer(d, block) * 2 + units[unit][2]) * size, 16), size)
+
+        def source_of(unit, block):
             which, plane, side = units[unit]
-            start = side * size if piece else (peer(d, block) * 2 + side) * size
-            return r[keys[which]].at[plane, pl.ds(pl.multiple_of(start, 16), size)]
+            rows = rows_of(unit, block) if summing else pl.ds(side * size, size)
+            return r[sources[which]].at[plane, rows]
+
+        def region(unit, block):
+            return r[gathered].at[flat.index(units[unit][:2]), rows_of(unit, block)]
 
         def swap(src, unit):
             mids[unit] = remote(
@@ -825,14 +897,14 @@
                 return
             side = units[unit][2]
             if not summing:
-                source = region(sources, unit, 0, True)
+                source = source_of(unit, 0)
                 swap(source.at[:, pl.ds(wide, wide)], unit)
                 loads[unit, 0] = local_copy(
-                    source.at[:, pl.ds(0, wide)], r[held].at[unit, 0], r[load_sems].at[unit, 0]
+                    source.at[:, pl.ds(0, wide)], region(unit, 0), r[load_sems].at[unit, 0]
                 )
                 return
             for block in range(n_dp):
-                source = region(sources, unit, block)
+                source = source_of(unit, block)
                 if block and stage(side, block) == 0:
                     send(source, unit, block)
                 else:
@@ -868,25 +940,47 @@
                     )
 
         def settle(unit):
-            total = r[mine][unit] if half and summing else summed(unit, 0)
+            place = region(unit, 0)
+            if half and summing:
+                total = r[mine][unit]
+            elif summing:
+                total = summed(unit, 0)
+            else:
+                loads[unit, 0].wait()
+                total = place[...].astype(F32)
             if half:
                 mids[unit].wait_recv()
                 total = total + r[given][unit].astype(F32)
-            r[final][unit] = total.astype(BF16)
-            place = region(targets, unit, 0)
-            keeps[unit] = local_copy(r[final].at[unit], place, r[keep_sems].at[unit])
-            spread(unit, 0, r[final].at[unit], place)
+            place[...] = total.astype(BF16)
+            spread(unit, 0, place, place)
 
         def onward(unit, level):
             for block in range(1, n_dp):
                 if level_of(block) == level:
                     spreads[unit, block].wait_recv()
-                    place = region(targets, unit, block)
+                    place = region(unit, block)
                     spread(unit, block, place, place)
+
+        def write(unit):
+            spreads[unit, n_dp - 1].wait_recv()
+            which, plane = target_of[flat.index(units[unit][:2])]
+            target = r[targets[which]]
+            for block in range(n_dp):
+                src = region(unit, block)
+                if outs[which]:
+                    to = target.at[plane, rows_of(unit, block)]
+                else:
+                    place = turned.index(unit)
+                    r[staged][place, block] = src[...].astype(F32).T.astype(BF16)
+                    src = r[staged].at[place, block]
+                    start = (peer(d, block) * 2 + units[unit][2]) * size
+                    to = target.at[:, pl.ds(pl.multiple_of(start, 128), size)]
+                keeps.append(local_copy(src, to, r[keep_sems].at[unit, block]))
 
         for unit in range(window):
             begin(unit)
-        first = depth if summing else 0
+        start = max(depth - 1, 0) if summing else 0
+        first = start + (1 if summing else 0) + (slack if half else 0)
         for step in range(count + first + depth):
             yield clock[0] + step * clock[1]
 
@@ -894,20 +988,66 @@
                 if 0 <= step - lag < count:
                     action(step - lag, *more)
 
+            turn(first + depth, write)
+
             for level in range(depth - 1, 0, -1):
                 turn(first + level, onward, level)
             turn(first, settle)
-            turn(max(first - 1, 0), cross)
+            turn(start, cross)
             if summing:
                 for level in range(depth - 1, 0, -1):
                     turn(level - 1, middle, level)
             begin(step + window)
-        for unit in range(count):
-            spreads[unit, n_dp - 1].wait_recv()
         for copy in [*sums.values(), *mids.values(), *spreads.values()]:
             copy.wait_send()
-        for copy in keeps.values():
+        for copy in keeps:
             copy.wait()
+
+    flow.steps = steps
+    return flow
+
+
+def dot_flow(left, right, turned=False, parts=8, clock=(4, 8)):
+    flow = Flow([])
+    high, deep = left.shape
+    wide = right.shape[0] if turned else right.shape[1]
+    part = high // parts
+    left_key, right_key = flow.take(left), flow.take(right)
+    result_key = flow.give((high, wide), BF16)
+    lefts, rights = flow.vmem(2, part, deep), flow.vmem(*right.shape)
+    results = flow.vmem(2, part, wide)
+    sems, right_sem = flow.sems(2, 2), flow.sems(1)
+
+    def steps(r):
+        loads, stores = {}, {}
+
+        def load(i):
+            if i < parts:
+                loads[i] = local_copy(
+                    r[left_key].at[pl.ds(i * part, part)], r[lefts].at[i % 2], r[sems].at[0, i % 2]
+                )
+
+        whole = local_copy(r[right_key], r[rights], r[right_sem].at[0])
+        load(0)
+        load(1)
+        for i in range(parts):
+            yield clock[0] + i * clock[1]
+            if i == 0:
+                whole.wait()
+            loads[i].wait()
+            if i > 1:
+                stores[i - 2].wait()
+            dims = (((1,), (1 if turned else 0,)), ((), ()))
+            value = lax.dot_general(
+                r[lefts][i % 2], r[rights][...], dims, preferred_element_type=F32
+            )
+            r[results][i % 2] = value.astype(BF16)
+            stores[i] = local_copy(
+                r[results].at[i % 2], r[result_key].at[pl.ds(i * part, part)], r[sems].at[1, i % 2]
+            )
+            load(i + 2)
+        for i in range(max(parts - 2, 0), parts):
+            stores[i].wait()
 
     flow.steps = steps
     return flow
@@ -979,7 +1119,7 @@
     live = (slot % CAP) < jnp.repeat(lengths, CAP)
     slot_row = jnp.where(live, slot // CAP, -1)[None, :]
 
-    (w_self2, w_self_out2), (n1,), (later,) = run_flows(
+    (w_self2, w_self_out2), (n1,), (later,), (text_columns,) = run_flows(
         0,
         "start",
         60,
@@ -988,13 +1128,13 @@
             image, norm_gains[0], norm_shifts[0], ag=half, keep=False, gather_clock=(12, 11)
         ),
         pass_flow(cotangent),
+        dot_flow(text, w_text),
     )
     w_self_out2 = w_self_out2[0]
     triple = planes_of(n1, w_self2)
     o1 = attend(seg_col, seg_row, (triple, 0), (triple, 1), (triple, 2))
     p1 = dot(o1, w_self_out2).astype(BF16)
     e3 = lax.all_gather(later, TENSOR, axis=0, tiled=True)
-    text_columns = dot(text, w_text).astype(BF16)
     (x1, n2), (w_kv2, w_cross_q2, w_cross_out2), (projected,) = run_flows(
         1,
         "self_sum",
@@ -1023,34 +1163,43 @@
     q2 = dot(n2, w_cross_q2).astype(BF16)
     o2 = attend(seg_col, slot_row, (q2, None), (pair, 0), (pair, 1))
     p2 = dot(o2, w_cross_out2).astype(BF16)
-    ((x2, n3),) = run_flows(
+    (x2, n3), (active_back,) = run_flows(
         2,
         "cross_sum",
         100,
-        stream_flow(x1, norm_gains[2], norm_shifts[2], terms=p2, rs=half, ag=n_tensor),
+        stream_flow(
+            x1,
+            norm_gains[2],
+            norm_shifts[2],
+            terms=p2,
+            rs=half,
+            ag=n_tensor,
+            clock=(5, 0, 6, 15),
+            gather_clock=(40, 6),
+        ),
+        dot_flow(e3, w_down, True, clock=(4, 11)),
     )
 
-    h = dot(n3, w_up)
-    act, slope = gelu_parts(h)
+    act, slope = gelu_parts(dot(n3, w_up))
     act = act.astype(BF16)
-    slope = slope.astype(BF16)
+    dh = (active_back.astype(F32) * slope).astype(BF16)
     down_grad = dot_t(act, e3).astype(BF16)
-    dh = (dot_r(e3, w_down) * slope.astype(F32)).astype(BF16)
     up_grad = dot_t(n3, dh).astype(BF16)
     sums = lax.psum((down_grad, up_grad), DP)
-    p3 = after(dot_r(dh, w_up).astype(BF16), down_grad, up_grad)
-    ((gain_two, shift_two, g2, e2),) = run_flows(
+    p3 = after(rows_dot([dh], w_up[None]), down_grad, up_grad)
+    (gain_two, shift_two, g2, e2), (p6,) = run_flows(
         3,
         "up_sum",
         100,
         stream_flow(
             x2, norm_gains[2], terms=p3, above=cotangent, rs=n_tensor, ag=half, clock=(8, 30, 6, 60)
         ),
+        dot_flow(act, w_down, clock=(12, 10)),
     )
 
     do2 = dot_r(e2, w_cross_out2).astype(BF16)
     dq2, dk2, dv2 = attend_back(seg_col, slot_row, (q2, None), (pair, 0), (pair, 1), do2)
-    p4 = dot_r(dq2, w_cross_q2).astype(BF16)
+    p4 = rows_dot([dq2], w_cross_q2[None])
     pair_back = jnp.stack([dk2, dv2])
     cross = jnp.concatenate(
         [
@@ -1060,7 +1209,7 @@
         ]
     )
     cross_part = lax.psum_scatter(cross, DP, scatter_dimension=1, tiled=True)
-    dproj = planes_back(pair_back, w_kv2)
+    dproj = rows_dot([dk2, dv2], w_kv2)
     (gain_one, shift_one, g1, e1), (dproj,) = run_flows(
         4,
         "query_sum",
@@ -1078,8 +1227,7 @@
         text_back_flow(dproj, half, n_tensor),
     )
 
-    p6 = dot(after(act, e1), w_down).astype(BF16)
-    down_sum = lax.psum_scatter(p6, TENSOR, scatter_dimension=0, tiled=True)
+    down_sum = lax.psum_scatter(after(p6, e1), TENSOR, scatter_dimension=0, tiled=True)
     image_out = (x2 + down_sum.astype(F32)).astype(BF16)
 
     do1 = dot_r(e1, w_self_out2).astype(BF16)
@@ -1088,15 +1236,21 @@
     own = planes_grad(n1, triple_back)
     own_out = dot_t(e1, o1).astype(BF16)[None]
     p5 = planes_back(triple_back, w_self2)
-    text_w_part = dot_t(text, dproj).astype(BF16)
-    p7 = dot_r(dproj, w_text).astype(BF16)
+    text_w_part = columns_dot(text, dproj)
+    p7 = rows_dot([dproj], w_text[None], 1024)
     everyone = [(TENSOR, bit) for bit in bits_of(n_tensor)] + [(DP, bit) for bit in bits_of(n_dp)]
     late = jnp.concatenate([gain_one, shift_one, gain_two, shift_two])
-    (own, own_out), (unused, unused, image_grad, all_sums), (text_grad,), (cross,), (text_w,) = run_flows(
+    (
+        (self_grad, self_out_grad),
+        (unused, unused, image_grad, all_sums),
+        (text_grad,),
+        (cross_q_grad, cross_kv_grad, cross_out_grad),
+        (text_w_grad,),
+    ) = run_flows(
         5,
         "end",
-        180,
-        grads_flow((own, own_out), n_dp, half, clock=(20, 20)),
+        200,
+        grads_flow((own, own_out), n_dp, (3, 0), half, clock=(14, 14)),
         stream_flow(
             image,
             norm_gains[0],
@@ -1109,17 +1263,14 @@
             clock=(6, 0, 8, 50),
         ),
         stream_flow(terms=p7, rs=n_tensor, keep=False, clock=(7, 45, 11, 110)),
-        grads_flow((cross_part,), n_dp, half, summing=False, clock=(15, 12)),
-        grads_flow((text_w_part.reshape(4, -1, width),), n_dp, clock=(10, 16)),
+        grads_flow((cross_part,), n_dp, (1, 2, 0), half, summing=False, clock=(15, 12)),
+        grads_flow((text_w_part.reshape(4, -1, width),), n_dp, (4,), clock=(10, 16)),
     )
-    self_grad = own.astype(F32)
-    self_out_grad = own_out[0].astype(F32).T
-    cross = cross.astype(F32)
-    cross_q_grad = cross[0]
-    cross_kv_grad = cross[1:3]
-    cross_out_grad = cross[3].T
-    text_w_grad = text_w.astype(F32).reshape(-1, width)
     down_grad, up_grad = [value.astype(F32) for value in sums]
+    self_grad, self_out_grad = self_grad.astype(F32), self_out_grad.astype(F32)
+    cross_q_grad, cross_kv_grad = cross_q_grad[0].astype(F32), cross_kv_grad.astype(F32)
+    cross_out_grad = cross_out_grad.astype(F32)
+    text_w_grad = text_w_grad.reshape(-1, width).astype(F32)
     gain_grad = jnp.stack([all_sums[4], all_sums[0], all_sums[2]])
     shift_grad = jnp.stack([all_sums[5], all_sums[1], all_sums[3]])
     return (

time: 1050 us -> 1010 us (0.962)
  matrix products: 177 us -> 105 us
  Pallas kernels: 791 us -> 836 us
  local copies, waits for them, and re-layouts: 24.5 us -> 13 us
    dot_general x6 -> x2, matrix products: 52.2 us -> 7.41 us  [dot_r(): lax.dot_general(left, right, (((1,), (1,)), ((), ())), preferred_element_...]
    pallas_call x0 -> x5, Pallas kernels: none -> 34.7 us  [the longest x4 26.7 us: rows_dot(): pl.pallas_call(functools.partial(rows_dot_kernel, count), grid=(wide // t...]
    pallas_call x6, Pallas kernels: 737 us -> 753 us  [run_flows(): pl.pallas_call(functools.partial(flows_kernel, flows), in_specs=[entry[1]...]
    dot_general x6 -> x4, matrix products: 47.8 us -> 33.5 us  [dot(): return jnp.dot(left, right, preferred_element_type=F32)]
    dot_general x6 -> x5, matrix products: 38.4 us -> 32 us  [dot_t(): lax.dot_general(left, right, (((0,), (0,)), ((), ())), preferred_element_...]
  transfers between devices with their start and end apart: 4 -> 4, of which waited for: 0 -> 0; matrix products, arithmetic and copies ran while one was open for 16% -> 9% of each run, Pallas kernels for 69% -> 63%
where the time goes in v2:
time: 1010 us; the launch traced here: 1000 us
  Pallas kernels  836 us (83%)
  matrix products  105 us (10%)
  other arithmetic  35 us (3%)
  between operations  14.6 us (1%)
  local copies, waits for them, and re-layouts  13 us (1%)
    pallas_call x6, Pallas kernels, run_flows(): pl.pallas_call(functools.partial(flows_kernel, flows), in_specs=[entry[1]...  753 us
    dot_general x4, matrix products, dot(): return jnp.dot(left, right, preferred_element_type=F32)  33.5 us
    dot_general x5, matrix products, dot_t(): lax.dot_general(left, right, (((0,), (0,)), ((), ())), preferred_element_...  32 us
    pallas_call x2, Pallas kernels, attend_back(): pl.pallas_call(functools.partial(attend_back_kernel, 256), grid=(heads,),...  30.4 us
    pallas_call x4, Pallas kernels, rows_dot(): pl.pallas_call(functools.partial(rows_dot_kernel, count), grid=(wide // t...  26.7 us
  transfers between devices with their start and end apart: 4, of which 0 were waited for; matrix products, arithmetic and copies ran while one was open for 9% of the time, Pallas kernels for 63%

profile of v2, /device:TPU:0, one launch (start us, length us, event | category | flops | bytes accessed | tf_op | source)
XLA Modules:
  0.0 1004.5 jit_solution(14740745909717761085)
XLA Ops:
  7.2 0.0 all-gather.2.cloned.1.call-start
  7.2 1.5 fusion.49
  8.8 71.3 %start.1 = (bf16[3,2048,512]{2,1,0:T(8,128)(2,1)}, bf16[1,512,2048]{2,1,0:T(8,128)(2,1)}, bf16[1024,2048]{1,0:T(8,128)(2,1)}, bf16[256,2048]{1,0:T(8,128)(2,1)}, bf16[1024,256]{1,0:T(8,128)(2,1)}) custom-call(bf16[3,2048,256]{2,1,0:T(8,128)(2,1)} %refs_0_.2, bf16[1,256,2048]{2,1,0:T(8,128)(2,1)} %bitcast.103, bf16[256,2048]{1,0:T(8,128)(2,1)} %refs_2_.5, ...), custom_call_target="tpu_custom_call" | custom-call | bytes 198000000 | tf_op jit(solution)/shard_map/start/pallas_call | solution.py:355
  80.1 0.0 all-gather.2.cloned.1.call-update
  80.2 0.1 reshape.103
  80.3 0.2 copy.41.qid_ref
  80.5 10.1 %convert_bitcast_fusion.2.q_ref.k_ref.v_ref = bf16[3,1024,512]{2,1,0:T(8,128)(2,1)S(1)} fusion(bf16[3,2048,512]{2,1,0:T(8,128)(2,1)} %get-tuple-element.52, bf16[1024,2048]{1,0:T(8,128)(2,1)} %get-tuple-element.53), kind=kOutput, calls=%fused_computation.24 | convolution fusion | flops 6444023808 | bytes 13631488 | tf_op jit(solution)/shard_map/td,cde->cte/dot_general | solution.py:215
  90.7 10.1 %attend.2 = bf16[1024,512]{1,0:T(8,128)(2,1)S(1)} custom-call(s32[1024,1]{1,0:T(8,128)S(1)} %copy.41.qid_ref, s32[1,1024]{1,0:T(1,128)S(1)} %constant_dynamic-slice_fusion.kid_ref, bf16[3,1024,512]{2,1,0:T(8,128)(2,1)S(1)} %convert_bitcast_fusion.2.q_ref.k_ref.v_ref, bf16[3,1024,512]{2,1,0:T(8,128)(2,1)S(1)} %convert_bitcast_fusion.2.q_ref.k_ref.v_ref, ...), custom_call_target="tpu_custom_call" | custom-call | flops 2147483648 | bytes 4194304 | tf_op jit(solution)/shard_map/attend/pallas_call | solution.py:88
  100.8 4.4 convolution_convert_fusion.2.refs_3_
  105.2 140.2 %self_sum.1 = (f32[256,2048]{1,0:T(8,128)}, bf16[1024,2048]{1,0:T(8,128)(2,1)}, bf16[2,2048,512]{2,1,0:T(8,128)(2,1)}, bf16[1,2048,512]{2,1,0:T(8,128)(2,1)}, bf...) custom-call(bf16[256,2048]{1,0:T(8,128)(2,1)} %refs_2_.5, f32[1,2048]{1,0:T(1,128)} %get-tuple-element.108.refs_1_, ...), custom_call_target="tpu_custom_call" | custom-call | bytes 330000000 | tf_op jit(solution)/shard_map/self_sum/pallas_call | solution.py:355
  245.5 0.1 broadcast_in_dim.38
  245.5 5.3 fusion.30.q_ref
  250.9 2.3 fusion.39.k_ref.v_ref
  253.3 7.4 attend.3
  260.7 4.4 convolution_convert_fusion.1.refs_3_
  265.1 114.6 %cross_sum.1 = (f32[256,2048]{1,0:T(8,128)}, bf16[2048,2048]{1,0:T(8,128)(2,1)}, bf16[2048,1024]{1,0:T(8,128)(2,1)}) custom-call(f32[256,2048]{1,0:T(8,128)} %get-tuple-element.56.refs_0_, f32[1,2048]{1,0:T(1,128)} %get-tuple-element.109.refs_1_, f32[1,2048]{1,0:T(1,128)} %get-tuple-element.101.refs_2_, ...), custom_call_target="tpu_custom_call" | custom-call | bytes 330000000 | tf_op jit(solution)/shard_map/cross_sum/pallas_call | solution.py:355
  379.7 19.4 %multiply_convert_fusion = (bf16[2048,1024]{1,0:T(8,128)(2,1)}, bf16[2048,1024]{1,0:T(8,128)(2,1)S(1)}) fusion(bf16[2048,1024]{1,0:T(8,128)(2,1)} %get-tuple-element.64, bf16[2048,2048]{1,0:T(8,128)(2,1)} %get-tuple-element.65, bf16[2048,1024]{1,0:T(8,128)(2,1)} %param.26), kind=kOutput, calls=%fused_computation.12 | convolution fusion | flops 8636071936 | bytes 25165824 | tf_op jit(solution)/shard_map/dot_general | solution.py:144
  399.1 10.8 %convolution_convert_fusion.3.refs_2_ = bf16[2048,1024]{1,0:T(8,128)(2,1)} fusion(bf16[2048,2048]{1,0:T(8,128)(2,1)S(1)} %copy-done.33, bf16[2048,1024]{1,0:T(8,128)(2,1)S(1)} %get-tuple-element.94.refs_0_), kind=kOutput, calls=%fused_computation.22 | convolution fusion | flops 8592031744 | bytes 16777216 | tf_op jit(solution)/shard_map/dot_general | solution.py:148
  410.0 12.6 %rows_dot.4.refs_0_ = bf16[2048,2048]{1,0:T(8,128)(2,1)} custom-call(bf16[2048,1024]{1,0:T(8,128)(2,1)S(1)} %get-tuple-element.94.refs_0_, bf16[1,2048,1024]{2,1,0:T(8,128)(2,1)} %bitcast.109), custom_call_target="tpu_custom_call" | custom-call | flops 8589934592 | bytes 16777216 | tf_op jit(solution)/shard_map/rows_dot/pallas_call | solution.py:169
  422.6 12.4 %convolution_convert_fusion.refs_1_ = bf16[1024,2048]{1,0:T(8,128)(2,1)} fusion(bf16[2048,1024]{1,0:T(8,128)(2,1)} %get-tuple-element.93.refs_4_, bf16[2048,2048]{1,0:T(8,128)(2,1)S(1)} %copy-done.20), kind=kOutput, calls=%fused_computation.19 | convolution fusion | flops 8592031744 | bytes 16777216 | tf_op jit(solution)/shard_map/dot_general | solution.py:148
  435.0 0.7 all-reduce.3.cloned.1.call-update
  435.7 0.4 reduce-scatter.5.cloned.1.call-start
  436.2 104.7 %up_sum.1 = (f32[1,2048]{1,0:T(1,128)}, f32[1,2048]{1,0:T(1,128)}, f32[256,2048]{1,0:T(8,128)}, bf16[1024,2048]{1,0:T(8,128)(2,1)}, bf16[2048,2048]{1,0:T(8,128)(2,1)}) custom-call(f32[256,2048]{1,0:T(8,128)} %get-tuple-element.63.refs_0_, f32[1,2048]{1,0:T(1,128)} %get-tuple-element.109.refs_1_, bf16[256,2048]{1,0:T(8,128)(2,1)} %refs_2_.4, ...), custom_call_target="tpu_custom_call" | custom-call | bytes 330000000 | tf_op jit(solution)/shard_map/up_sum/pallas_call | solution.py:355
  540.9 5.1 fusion.36.do_ref
  546.0 11.2 %attend_back.2 = (bf16[1024,512]{1,0:T(8,128)(2,1)S(1)}, bf16[512,512]{1,0:T(8,128)(2,1)S(1)}, bf16[512,512]{1,0:T(8,128)(2,1)S(1)}) custom-call(s32[1024,1]{1,0:T(8,128)S(1)} %copy.41.qid_ref, s32[1,512]{1,0:T(1,128)S(1)} %compare_select_fusion.kid_ref, bf16[1024,512]{1,0:T(8,128)(2,1)S(1)} %copy-done.10, bf16[2,512,512]{2,1,0:T(8,128)(2,1)S(1)} %fusion.39.k_ref.v_ref, ...), custom_call_target="tpu_custom_call" | custom-call | flops 2684354560 | bytes 5242880 | tf_op jit(solution)/shard_map/attend_back/pallas_call | solution.py:115
  557.2 2.4 convert_bitcast_fusion.1
  559.6 0.3 copy-done.36
  559.9 2.4 fusion.12
  562.4 2.5 fusion.11
  564.9 3.8 pad_maximum_fusion.refs_1_
  568.7 0.3 reduce-scatter.3.cloned.1.call-start
  569.0 1.3 copy-done.15
  570.3 1.2 copy-done.17
  571.5 4.2 rows_dot.5.refs_0_
  575.7 1.1 copy-done.12
  576.8 4.9 rows_dot.6.refs_4_
  581.6 1.3 copy-done.5
  582.9 72.7 %query_sum.1 = (f32[1,2048]{1,0:T(1,128)}, f32[1,2048]{1,0:T(1,128)}, f32[256,2048]{1,0:T(8,128)}, bf16[1024,2048]{1,0:T(8,128)(2,1)}, bf16[1024,256]{1,0:T(8,128)(2,1)}) custom-call(f32[256,2048]{1,0:T(8,128)} %get-tuple-element.56.refs_0_, f32[1,2048]{1,0:T(1,128)} %get-tuple-element.108.refs_1_, f32[256,2048]{1,0:T(8,128)} %get-tuple-element.67.refs_2_, ...), custom_call_target="tpu_custom_call" | custom-call | bytes 198000000 | tf_op jit(solution)/shard_map/query_sum/pallas_call | solution.py:355
  655.7 0.0 reduce-scatter.3.cloned.1.call-update
  655.7 1.0 copy-done.6
  656.7 8.0 columns_dot.1
  664.7 1.3 copy-done.4
  666.1 5.1 rows_dot.7.refs_7_
  671.2 0.7 pad_maximum_fusion.4.refs_6_
  671.8 2.4 fusion.27.do_ref
  674.2 19.2 %attend_back.3 = (bf16[1024,512]{1,0:T(8,128)(2,1)S(1)}, bf16[1024,512]{1,0:T(8,128)(2,1)S(1)}, bf16[1024,512]{1,0:T(8,128)(2,1)S(1)}) custom-call(s32[1024,1]{1,0:T(8,128)S(1)} %copy.41.qid_ref, s32[1,1024]{1,0:T(1,128)S(1)} %copy-done.14, bf16[3,1024,512]{2,1,0:T(8,128)(2,1)} %copy-done.2, bf16[3,1024,512]{2,1,0:T(8,128)(2,1)} %copy-done.2, ...), custom_call_target="tpu_custom_call" | custom-call | flops 5368709120 | bytes 7340032 | tf_op jit(solution)/shard_map/attend_back/pallas_call | solution.py:115
  693.5 3.8 fusion.13.refs_1_
  697.3 8.8 convert_bitcast_fusion.refs_0_
  706.0 8.4 bitcast_convert_fusion.refs_5_
  714.4 0.0 all-reduce.3.cloned.1.call-done
  714.5 6.8 convert_element_type.131
  721.3 4.5 convert_element_type.132
  725.7 249.3 %end.1 = (bf16[3,2048,256]{2,1,0:T(8,128)(2,1)}, bf16[256,2048]{1,0:T(8,128)(2,1)}, f32[1,2048]{1,0:T(1,128)}, f32[1,2048]{1,0:T(1,128)}, bf16[256,2048]{1,0:T(8...) custom-call(bf16[3,2048,512]{2,1,0:T(8,128)(2,1)} %convert_bitcast_f, ...), custom_call_target="tpu_custom_call" | custom-call | bytes 660000000 | tf_op jit(solution)/shard_map/end/pallas_call | solution.py:355
  975.1 2.9 convert_element_type.124
  978.0 2.9 convert_element_type.128
  980.9 2.3 convert_element_type.127
  983.3 3.2 convert_element_type.123
  986.6 0.6 pad_maximum_fusion.6
  987.2 0.6 pad_maximum_fusion.5
  987.9 1.5 bitcast_convert_fusion.2
  989.4 2.5 bitcast_convert_fusion.1
  991.8 2.6 add_convert_fusion
  994.5 2.3 copy.66
  996.8 1.0 copy.67
  (99 shorter events, 0.3 us)
Async XLA Ops:
  7.2 73.1 %copy-start = (s32[2,1024]{1,0:T(2,128)S(1)}, s32[2,1024]{1,0:T(2,128)}, u32[]{:S(2)}) copy-start(s32[2,1024]{1,0:T(2,128)} %param.28) | copy-start | bytes 24580
  7.2 257.9 %all-gather.2.cloned.1.call-start = ((), (), s32[]{:S(2)}) async-start(), calls=%async_computation.2 | async-start | bytes 9437184 | tf_op jit(solution)/shard_map/all_gather | solution.py:1137
  8.8 71.4 %copy-start.43 = (s32[8]{0:T(128)S(1)}, s32[8]{0:T(128)}, u32[]{:S(2)}) copy-start(s32[8]{0:T(128)} %param.29) | copy-start | bytes 100
  80.5 10.1 %copy-start.13 = (s32[1,1024]{1,0:T(1,128)}, s32[1,1024]{1,0:T(1,128)S(1)}, u32[]{:S(2)}) copy-start(s32[1,1024]{1,0:T(1,128)S(1)} %constant_dynamic-slice_fusion.kid_ref) | copy-start | bytes 12292
  90.7 10.2 %copy-start.2 = (bf16[3,1024,512]{2,1,0:T(8,128)(2,1)}, bf16[3,1024,512]{2,1,0:T(8,128)(2,1)S(1)}, u32[]{:S(2)}) copy-start(bf16[3,1024,512]{2,1,0:T(8,128)(2,1)S(1)} %convert_bitcast_fusion.2.q_ref.k_ref.v_ref) | copy-start | bytes 9437188
  90.7 10.2 %copy-start.37 = (bf16[1,512,2048]{2,1,0:T(8,128)(2,1)S(1)}, bf16[1,512,2048]{2,1,0:T(8,128)(2,1)}, u32[]{:S(2)}) copy-start(bf16[1,512,2048]{2,1,0:T(8,128)(2,1)} %get-tuple-element.54) | copy-start | bytes 6291460
  100.8 4.4 copy-start.7
  245.5 5.4 copy-start.18
  245.5 5.4 copy-start.39
  250.9 2.4 copy-start.9
  253.2 7.5 copy-start.41
  379.7 19.4 %copy-start.33 = (bf16[2048,2048]{1,0:T(8,128)(2,1)S(1)}, bf16[2048,2048]{1,0:T(8,128)(2,1)}, u32[]{:S(2)}) copy-start(bf16[2048,2048]{1,0:T(8,128)(2,1)} %get-tuple-element.65) | copy-start | bytes 25165828
  410.0 12.6 %copy-start.20 = (bf16[2048,2048]{1,0:T(8,128)(2,1)S(1)}, bf16[2048,2048]{1,0:T(8,128)(2,1)}, u32[]{:S(2)}) copy-start(bf16[2048,2048]{1,0:T(8,128)(2,1)} %all-gather.2.cloned.1.call-done.refs_4_) | copy-start | bytes 25165828
  435.0 279.5 %all-reduce.3.cloned.1.call-start = ((), (), s32[]{:S(2)}) async-start(), calls=%async_computation.5 | async-start | bytes 16777216 | tf_op jit(solution)/shard_map/psum | solution.py:1188
  435.7 290.0 %reduce-scatter.5.cloned.1.call-start = ((), (), s32[]{:S(2)}) async-start(), calls=%async_computation.4 | async-start | bytes 10485760 | tf_op jit(solution)/shard_map/reduce_scatter | solution.py:1211
  436.2 104.7 %copy-start.42 = (bf16[1,512,2048]{2,1,0:T(8,128)(2,1)S(1)}, bf16[1,512,2048]{2,1,0:T(8,128)(2,1)}, u32[]{:S(2)}) copy-start(bf16[1,512,2048]{2,1,0:T(8,128)(2,1)} %get-tuple-element.61) | copy-start | bytes 6291460
  540.9 5.1 copy-start.10
  546.0 11.2 %copy-start.40 = (bf16[512,2048]{1,0:T(8,128)(2,1)S(1)}, bf16[512,2048]{1,0:T(8,128)(2,1)}, u32[]{:S(2)}) copy-start(bf16[512,2048]{1,0:T(8,128)(2,1)} %get-tuple-element.60) | copy-start | bytes 6291460
  557.2 2.5 copy-start.11
  557.2 5.2 copy-start.16
  557.2 2.7 copy-start.36
  559.9 2.5 copy-start.35
  568.7 1.6 copy-start.15
  568.7 423.1 %reduce-scatter.3.cloned.1.call-start = ((), (), s32[]{:S(2)}) async-start(), calls=%async_computation.3 | async-start | bytes 9437184 | tf_op jit(solution)/shard_map/reduce_scatter | solution.py:1230
  570.3 1.2 copy-start.17
  575.7 1.1 copy-start.12
  581.6 1.3 copy-start.5
  655.7 1.0 copy-start.6
  656.7 9.3 copy-start.3
  664.7 1.3 copy-start.4
  666.0 5.1 copy-start.29
  666.1 5.1 copy-start.30
  666.1 5.1 copy-start.31
  666.1 5.1 copy-start.32
  666.1 5.8 copy-start.22
  666.1 5.7 copy-start.38
  671.8 2.4 copy-start.14
  674.2 19.3 %copy-start.8 = (bf16[1024,512]{1,0:T(8,128)(2,1)S(1)}, bf16[1024,512]{1,0:T(8,128)(2,1)}, u32[]{:S(2)}) copy-start(bf16[1024,512]{1,0:T(8,128)(2,1)} %copy-done.7) | copy-start | bytes 3145732
  693.5 3.8 copy-start.34
  693.5 12.5 %slice-start = ((s8[6291456]{0:T(1024)(128)(4,1)}), s8[4194304]{0:T(1024)(128)(4,1)S(1)}, s32[]{:S(2)}) async-start(s8[6291456]{0:T(1024)(128)(4,1)} %bitcast.107), calls=%async_computation.6 | async-start | bytes 8388608
  697.3 8.8 slice-start.1
  714.5 6.8 copy-start.21
  975.1 5.9 copy-start.25
  978.0 5.3 copy-start.23
  983.3 3.3 copy-start.28
  983.3 4.6 copy-start.26
  983.3 6.1 copy-start.24
  987.9 4.0 copy-start.19
  989.4 8.4 copy-start.1
  991.8 4.9 copy-start.27
Sparse Core Ops, SparseCore 0:
  80.3 122.8 all-gather.1
  440.2 171.8 all-reduce.2
  615.4 87.1 reduce-scatter.4
  704.7 166.0 reduce-scatter.2

commit v3 on v2

--- a/solution.py
+++ b/solution.py
@@ -238,6 +238,37 @@
     half = 0.5 * (1.0 + th)
     slope = half + 0.5 * h * (1.0 - th * th) * (c * (1.0 + 3 * 0.044715 * h * h))
     return h * half, slope
+
+
+def hidden_kernel(tokens_ref, weight_ref, back_ref, act_ref, out_ref):
+    h = jnp.dot(tokens_ref[...], weight_ref[...], preferred_element_type=F32)
+    act, slope = gelu_parts(h)
+    act_ref[...] = act.astype(BF16)
+    out_ref[...] = (back_ref[...].astype(F32) * slope).astype(BF16)
+
+
+def hidden_step(tokens, weight, back, tile=256):
+    high, deep = tokens.shape
+    wide = weight.shape[1]
+    part = pl.BlockSpec((tile, wide), lambda m: (m, 0))
+    return pl.pallas_call(
+        hidden_kernel,
+        grid=(high // tile,),
+        in_specs=[
+            pl.BlockSpec((tile, deep), lambda m: (m, 0)),
+            pl.BlockSpec((deep, wide), lambda m: (0, 0)),
+            part,
+        ],
+        out_specs=[part, part],
+        out_shape=[jax.ShapeDtypeStruct((high, wide), BF16)] * 2,
+        compiler_params=pltpu.CompilerParams(vmem_limit_bytes=48 * MIB),
+        cost_estimate=pl.CostEstimate(
+            flops=2 * high * deep * wide,
+            bytes_accessed=2 * (high * deep + deep * wide + 3 * high * wide),
+            transcendentals=high * wide,
+        ),
+        name="hidden_step",
+    )(tokens, weight, back)
 
 
 def partner(index, bit):
@@ -1180,9 +1211,7 @@
         dot_flow(e3, w_down, True, clock=(4, 11)),
     )
 
-    act, slope = gelu_parts(dot(n3, w_up))
-    act = act.astype(BF16)
-    dh = (active_back.astype(F32) * slope).astype(BF16)
+    act, dh = hidden_step(n3, w_up, active_back)
     down_grad = dot_t(act, e3).astype(BF16)
     up_grad = dot_t(n3, dh).astype(BF16)
     sums = lax.psum((down_grad, up_grad), DP)
@@ -1238,12 +1267,12 @@
     p5 = planes_back(triple_back, w_self2)
     text_w_part = columns_dot(text, dproj)
     p7 = rows_dot([dproj], w_text[None], 1024)
+    text_grad = lax.psum_scatter(p7, TENSOR, scatter_dimension=0, tiled=True)
     everyone = [(TENSOR, bit) for bit in bits_of(n_tensor)] + [(DP, bit) for bit in bits_of(n_dp)]
     late = jnp.concatenate([gain_one, shift_one, gain_two, shift_two])
     (
         (self_grad, self_out_grad),
         (unused, unused, image_grad, all_sums),
-        (text_grad,),
         (cross_q_grad, cross_kv_grad, cross_out_grad),
         (text_w_grad,),
     ) = run_flows(
@@ -1262,7 +1291,6 @@
             everyone=everyone,
             clock=(6, 0, 8, 50),
         ),
-        stream_flow(terms=p7, rs=n_tensor, keep=False, clock=(7, 45, 11, 110)),
         grads_flow((cross_part,), n_dp, (1, 2, 0), half, summing=False, clock=(15, 12)),
         grads_flow((text_w_part.reshape(4, -1, width),), n_dp, (4,), clock=(10, 16)),
     )

time: 1010 us -> 992 us (0.982)
  Pallas kernels: 836 us -> 800 us
  waiting for transfers between devices: 0.8 us -> 30 us
  matrix products: 105 us -> 91.2 us
    pallas_call x6, Pallas kernels: 753 us -> 698 us  [run_flows(): pl.pallas_call(functools.partial(flows_kernel, flows), in_specs=[entry[1]...]
    reduce_scatter x0 -> x1, waiting for transfers between devices: none -> 29.2 us  [local(): text_grad = lax.psum_scatter(p7, TENSOR, scatter_dimension=0, tiled=True)]
    dot_general x4 -> x3, matrix products: 33.5 us -> 14 us  [dot(): return jnp.dot(left, right, preferred_element_type=F32)]
    pallas_call x0 -> x1, Pallas kernels: none -> 19.1 us  [hidden_step(): pl.pallas_call(hidden_kernel, grid=(high // tile,), in_specs=[pl.BlockSpe...]
  transfers between devices with their start and end apart: 4 -> 5, of which waited for: 0 -> 1; matrix products, arithmetic and copies ran while one was open for 9% -> 10% of each run, Pallas kernels for 63% -> 59%
where the time goes in v3:
time: 992 us; the launch traced here: 984 us
  Pallas kernels  800 us (81%)
  matrix products  91.2 us (9%)
  other arithmetic  35.3 us (4%)
  waiting for transfers between devices  30 us (3%)
  between operations  14.8 us (1%)
  local copies, waits for them, and re-layouts  12.2 us (1%)
    pallas_call x6, Pallas kernels, run_flows(): pl.pallas_call(functools.partial(flows_kernel, flows), in_specs=[entry[1]...  698 us
    dot_general x5, matrix products, dot_t(): lax.dot_general(left, right, (((0,), (0,)), ((), ())), preferred_element_...  37.2 us
    pallas_call x2, Pallas kernels, attend_back(): pl.pallas_call(functools.partial(attend_back_kernel, 256), grid=(heads,),...  30.4 us
    reduce_scatter x1, waiting for transfers between devices, local(): text_grad = lax.psum_scatter(p7, TENSOR, scatter_dimension=0, tiled=True)  29.2 us
    pallas_call x4, Pallas kernels, rows_dot(): pl.pallas_call(functools.partial(rows_dot_kernel, count), grid=(wide // t...  26.4 us
  transfers between devices with their start and end apart: 5, of which 1 were waited for; matrix products, arithmetic and copies ran while one was open for 10% of the time, Pallas kernels for 59%

profile of v3, /device:TPU:0, one launch (start us, length us, event | category | flops | bytes accessed | tf_op | source)
XLA Modules:
  0.0 983.7 jit_solution(119588404327513979)
XLA Ops:
  7.2 0.0 all-gather.2.cloned.1.call-start
  7.2 1.5 fusion.41
  8.8 71.3 %start.1 = (bf16[3,2048,512]{2,1,0:T(8,128)(2,1)}, bf16[1,512,2048]{2,1,0:T(8,128)(2,1)}, bf16[1024,2048]{1,0:T(8,128)(2,1)}, bf16[256,2048]{1,0:T(8,128)(2,1)}, bf16[1024,256]{1,0:T(8,128)(2,1)}) custom-call(bf16[3,2048,256]{2,1,0:T(8,128)(2,1)} %refs_0_.2, bf16[1,256,2048]{2,1,0:T(8,128)(2,1)} %bitcast.101, bf16[256,2048]{1,0:T(8,128)(2,1)} %refs_2_.5, ...), custom_call_target="tpu_custom_call" | custom-call | bytes 198000000 | tf_op jit(solution)/shard_map/start/pallas_call | solution.py:386
  80.1 0.0 all-gather.2.cloned.1.call-update
  80.2 0.1 reshape.103
  80.3 1.0 copy.41.qid_ref
  81.3 10.2 %convert_bitcast_fusion.2.q_ref.k_ref.v_ref = bf16[3,1024,512]{2,1,0:T(8,128)(2,1)S(1)} fusion(bf16[3,2048,512]{2,1,0:T(8,128)(2,1)} %get-tuple-element.53, bf16[1024,2048]{1,0:T(8,128)(2,1)} %get-tuple-element.54), kind=kOutput, calls=%fused_computation.12 | convolution fusion | flops 6444023808 | bytes 13631488 | tf_op jit(solution)/shard_map/td,cde->cte/dot_general | solution.py:215
  91.5 10.1 %attend.2 = bf16[1024,512]{1,0:T(8,128)(2,1)S(1)} custom-call(s32[1024,1]{1,0:T(8,128)S(1)} %copy-done.6, s32[1,1024]{1,0:T(1,128)S(1)} %constant_dynamic-slice_fusion.kid_ref, bf16[3,1024,512]{2,1,0:T(8,128)(2,1)S(1)} %convert_bitcast_fusion.2.q_ref.k_ref.v_ref, bf16[3,1024,512]{2,1,0:T(8,128)(2,1)S(1)} %convert_bitcast_fusion.2.q_ref.k_ref.v_ref, ...), custom_call_target="tpu_custom_call" | custom-call | flops 2147483648 | bytes 4194304 | tf_op jit(solution)/shard_map/attend/pallas_call | solution.py:88
  101.7 4.4 convolution_convert_fusion.2.refs_3_
  106.0 139.5 %self_sum.1 = (f32[256,2048]{1,0:T(8,128)}, bf16[1024,2048]{1,0:T(8,128)(2,1)}, bf16[2,2048,512]{2,1,0:T(8,128)(2,1)}, bf16[1,2048,512]{2,1,0:T(8,128)(2,1)}, bf...) custom-call(bf16[256,2048]{1,0:T(8,128)(2,1)} %refs_2_.5, f32[1,2048]{1,0:T(1,128)} %get-tuple-element.108.refs_1_, ...), custom_call_target="tpu_custom_call" | custom-call | bytes 330000000 | tf_op jit(solution)/shard_map/self_sum/pallas_call | solution.py:386
  245.5 0.1 broadcast_in_dim.38
  245.6 5.3 fusion.22.q_ref
  251.0 2.3 fusion.31.k_ref.v_ref
  253.3 7.4 attend.3
  260.7 4.4 convolution_convert_fusion.1.refs_3_
  265.1 114.6 %cross_sum.1 = (f32[256,2048]{1,0:T(8,128)}, bf16[2048,2048]{1,0:T(8,128)(2,1)}, bf16[2048,1024]{1,0:T(8,128)(2,1)}) custom-call(f32[256,2048]{1,0:T(8,128)} %get-tuple-element.57.refs_0_, f32[1,2048]{1,0:T(1,128)} %get-tuple-element.109.refs_1_, f32[1,2048]{1,0:T(1,128)} %get-tuple-element.101.refs_2_, ...), custom_call_target="tpu_custom_call" | custom-call | bytes 330000000 | tf_op jit(solution)/shard_map/cross_sum/pallas_call | solution.py:386
  379.7 19.1 %hidden_step.1 = (bf16[2048,1024]{1,0:T(8,128)(2,1)S(1)}, bf16[2048,1024]{1,0:T(8,128)(2,1)}) custom-call(bf16[2048,2048]{1,0:T(8,128)(2,1)} %get-tuple-element.65.tokens_ref, bf16[2048,1024]{1,0:T(8,128)(2,1)} %weight_ref.1, bf16[2048,1024]{1,0:T(8,128)(2,1)} %get-tuple-element.66.back_ref), custom_call_target="tpu_custom_call" | custom-call | flops 8589934592 | bytes 25165824 | tf_op jit(solution)/shard_map/hidden_step/pallas_call | solution.py:254
  398.8 15.5 %convolution_convert_fusion.3.refs_2_ = bf16[2048,1024]{1,0:T(8,128)(2,1)} fusion(bf16[2048,2048]{1,0:T(8,128)(2,1)} %get-tuple-element.65.tokens_ref, bf16[2048,1024]{1,0:T(8,128)(2,1)} %get-tuple-element.67.refs_0_), kind=kOutput, calls=%fused_computation.10 | convolution fusion | flops 8592031744 | bytes 16777216 | tf_op jit(solution)/shard_map/dot_general | solution.py:148
  414.3 12.4 %rows_dot.4.refs_0_ = bf16[2048,2048]{1,0:T(8,128)(2,1)} custom-call(bf16[2048,1024]{1,0:T(8,128)(2,1)S(1)} %copy-done.19, bf16[1,2048,1024]{2,1,0:T(8,128)(2,1)} %bitcast.107), custom_call_target="tpu_custom_call" | custom-call | flops 8589934592 | bytes 16777216 | tf_op jit(solution)/shard_map/rows_dot/pallas_call | solution.py:169
  426.7 13.0 %convolution_convert_fusion.refs_1_ = bf16[1024,2048]{1,0:T(8,128)(2,1)} fusion(bf16[2048,1024]{1,0:T(8,128)(2,1)S(1)} %get-tuple-element.68.refs_4_, bf16[2048,2048]{1,0:T(8,128)(2,1)} %all-gather.2.cloned.1.call-done.refs_4_), kind=kOutput, calls=%fused_computation.7 | convolution fusion | flops 8592031744 | bytes 16777216 | tf_op jit(solution)/shard_map/dot_general | solution.py:148
  439.7 0.7 all-reduce.3.cloned.1.call-update
  440.4 0.3 reduce-scatter.6.cloned.1.call-start
  440.7 104.7 %up_sum.1 = (f32[1,2048]{1,0:T(1,128)}, f32[1,2048]{1,0:T(1,128)}, f32[256,2048]{1,0:T(8,128)}, bf16[1024,2048]{1,0:T(8,128)(2,1)}, bf16[2048,2048]{1,0:T(8,128)(2,1)}) custom-call(f32[256,2048]{1,0:T(8,128)} %get-tuple-element.64.refs_0_, f32[1,2048]{1,0:T(1,128)} %get-tuple-element.109.refs_1_, bf16[256,2048]{1,0:T(8,128)(2,1)} %refs_2_.4, ...), custom_call_target="tpu_custom_call" | custom-call | bytes 330000000 | tf_op jit(solution)/shard_map/up_sum/pallas_call | solution.py:386
  545.4 5.4 fusion.28.do_ref
  550.8 11.2 %attend_back.2 = (bf16[1024,512]{1,0:T(8,128)(2,1)S(1)}, bf16[512,512]{1,0:T(8,128)(2,1)S(1)}, bf16[512,512]{1,0:T(8,128)(2,1)S(1)}) custom-call(s32[1024,1]{1,0:T(8,128)S(1)} %copy-done.7, s32[1,512]{1,0:T(1,128)S(1)} %compare_select_fusion.kid_ref, bf16[1024,512]{1,0:T(8,128)(2,1)S(1)} %copy-done.13, bf16[2,512,512]{2,1,0:T(8,128)(2,1)S(1)} %fusion.31.k_ref.v_ref, ...), custom_call_target="tpu_custom_call" | custom-call | flops 2684354560 | bytes 5242880 | tf_op jit(solution)/shard_map/attend_back/pallas_call | solution.py:115
  562.1 2.4 convert_bitcast_fusion.1
  564.5 0.3 copy-done.36
  564.8 2.5 fusion.4
  567.3 2.5 fusion.3
  569.8 4.0 pad_maximum_fusion.refs_1_
  573.8 0.2 reduce-scatter.4.cloned.1.call-start
  574.0 1.3 copy-done.16
  575.3 1.2 copy-done.18
  576.6 4.2 rows_dot.5.refs_0_
  580.7 1.1 copy-done.15
  581.8 4.8 rows_dot.6.refs_4_
  586.7 1.3 copy-done.5
  588.0 72.6 %query_sum.1 = (f32[1,2048]{1,0:T(1,128)}, f32[1,2048]{1,0:T(1,128)}, f32[256,2048]{1,0:T(8,128)}, bf16[1024,2048]{1,0:T(8,128)(2,1)}, bf16[1024,256]{1,0:T(8,128)(2,1)}) custom-call(f32[256,2048]{1,0:T(8,128)} %get-tuple-element.57.refs_0_, f32[1,2048]{1,0:T(1,128)} %get-tuple-element.108.refs_1_, f32[256,2048]{1,0:T(8,128)} %get-tuple-element.70.refs_2_, ...), custom_call_target="tpu_custom_call" | custom-call | bytes 198000000 | tf_op jit(solution)/shard_map/query_sum/pallas_call | solution.py:386
  660.7 0.0 reduce-scatter.8.cloned.1.call-start
  660.7 1.5 copy-done.3
  662.2 0.1 copy-done.9
  662.4 5.0 rows_dot.7
  667.5 8.5 columns_dot.1
  676.0 1.3 copy-done.4
  677.3 0.7 pad_maximum_fusion.4.refs_6_
  678.0 2.4 fusion.19.do_ref
  680.4 19.2 %attend_back.3 = (bf16[1024,512]{1,0:T(8,128)(2,1)S(1)}, bf16[1024,512]{1,0:T(8,128)(2,1)S(1)}, bf16[1024,512]{1,0:T(8,128)(2,1)S(1)}) custom-call(s32[1024,1]{1,0:T(8,128)S(1)} %copy-done.7, s32[1,1024]{1,0:T(1,128)S(1)} %constant_dynamic-slice_fusion.kid_ref, bf16[3,1024,512]{2,1,0:T(8,128)(2,1)} %copy-done.2, bf16[3,1024,512]{2,1,0:T(8,128)(2,1)} %copy-done.2, ...), custom_call_target="tpu_custom_call" | custom-call | flops 5368709120 | bytes 7340032 | tf_op jit(solution)/shard_map/attend_back/pallas_call | solution.py:115
  699.6 3.8 fusion.5.refs_1_
  703.4 9.0 convert_bitcast_fusion.refs_0_
  712.3 8.3 bitcast_convert_fusion.refs_5_
  720.6 6.8 convert_element_type.119
  727.4 4.5 convert_element_type.120
  731.9 195.2 %end.1 = (bf16[3,2048,256]{2,1,0:T(8,128)(2,1)}, bf16[256,2048]{1,0:T(8,128)(2,1)}, f32[1,2048]{1,0:T(1,128)}, f32[1,2048]{1,0:T(1,128)}, bf16[256,2048]{1,0:T(8...) custom-call(bf16[3,2048,512]{2,1,0:T(8,128)(2,1)} %convert_bitcast_f, ...), custom_call_target="tpu_custom_call" | custom-call | bytes 660000000 | tf_op jit(solution)/shard_map/end/pallas_call | solution.py:386
  927.1 3.0 convert_element_type.112
  930.1 3.0 convert_element_type.116
  933.1 2.3 convert_element_type.115
  935.4 3.2 convert_element_type.111
  938.7 0.6 pad_maximum_fusion.6
  939.4 0.6 pad_maximum_fusion.5
  940.0 1.5 bitcast_convert_fusion.2
  941.5 2.7 add_convert_fusion
  944.2 2.5 bitcast_convert_fusion.1
  946.7 29.2 %reduce-scatter.8.cloned.1.call-done = bf16[128,4096]{1,0:T(8,128)(2,1)} async-done(((bf16[1024,4096]{1,0:T(8,128)(2,1)}), bf16[128,4096]{1,0:T(8,128)(2,1)}) %reduce-scatter.8.cloned.1.call-update) | async-done | bytes 1048592 | tf_op jit(solution)/shard_map/reduce_scatter | solution.py:1270
  975.9 1.0 copy.65
  (101 shorter events, 0.3 us)
Async XLA Ops:
  7.2 73.1 %copy-start = (s32[2,1024]{1,0:T(2,128)S(1)}, s32[2,1024]{1,0:T(2,128)}, u32[]{:S(2)}) copy-start(s32[2,1024]{1,0:T(2,128)} %param.28) | copy-start | bytes 24580
  7.2 257.9 %all-gather.2.cloned.1.call-start = ((), (), s32[]{:S(2)}) async-start(), calls=%async_computation.3 | async-start | bytes 9437184 | tf_op jit(solution)/shard_map/all_gather | solution.py:1168
  8.8 71.4 %copy-start.43 = (s32[8]{0:T(128)S(1)}, s32[8]{0:T(128)}, u32[]{:S(2)}) copy-start(s32[8]{0:T(128)} %param.29) | copy-start | bytes 100
  81.3 10.2 %copy-start.6 = (s32[1024,1]{1,0:T(8,128)S(1)}, s32[1024,1]{1,0:T(8,128)}, u32[]{:S(2)}) copy-start(s32[1024,1]{1,0:T(8,128)} %copy.41.qid_ref) | copy-start | bytes 12292
  91.5 10.1 %copy-start.2 = (bf16[3,1024,512]{2,1,0:T(8,128)(2,1)}, bf16[3,1024,512]{2,1,0:T(8,128)(2,1)S(1)}, u32[]{:S(2)}) copy-start(bf16[3,1024,512]{2,1,0:T(8,128)(2,1)S(1)} %convert_bitcast_fusion.2.q_ref.k_ref.v_ref) | copy-start | bytes 9437188
  91.5 10.2 %copy-start.37 = (bf16[1,512,2048]{2,1,0:T(8,128)(2,1)S(1)}, bf16[1,512,2048]{2,1,0:T(8,128)(2,1)}, u32[]{:S(2)}) copy-start(bf16[1,512,2048]{2,1,0:T(8,128)(2,1)} %get-tuple-element.55) | copy-start | bytes 6291460
  101.6 4.4 copy-start.10
  245.6 5.4 copy-start.20
  245.6 5.4 copy-start.39
  251.0 2.4 copy-start.12
  253.3 7.4 copy-start.41
  398.7 27.9 %copy-start.8 = (bf16[2048,1024]{1,0:T(8,128)(2,1)}, bf16[2048,1024]{1,0:T(8,128)(2,1)S(1)}, u32[]{:S(2)}) copy-start(bf16[2048,1024]{1,0:T(8,128)(2,1)S(1)} %get-tuple-element.68.refs_4_) | copy-start | bytes 12582916
  398.8 15.5 %copy-start.19 = (bf16[2048,1024]{1,0:T(8,128)(2,1)S(1)}, bf16[2048,1024]{1,0:T(8,128)(2,1)}, u32[]{:S(2)}) copy-start(bf16[2048,1024]{1,0:T(8,128)(2,1)} %get-tuple-element.67.refs_0_) | copy-start | bytes 12582916
  439.7 281.0 %all-reduce.3.cloned.1.call-start = ((), (), s32[]{:S(2)}) async-start(), calls=%async_computation.7 | async-start | bytes 16777216 | tf_op jit(solution)/shard_map/psum | solution.py:1217
  440.4 291.5 %reduce-scatter.6.cloned.1.call-start = ((), (), s32[]{:S(2)}) async-start(), calls=%async_computation.5 | async-start | bytes 10485760 | tf_op jit(solution)/shard_map/reduce_scatter | solution.py:1240
  440.7 104.7 %copy-start.42 = (bf16[1,512,2048]{2,1,0:T(8,128)(2,1)S(1)}, bf16[1,512,2048]{2,1,0:T(8,128)(2,1)}, u32[]{:S(2)}) copy-start(bf16[1,512,2048]{2,1,0:T(8,128)(2,1)} %get-tuple-element.62) | copy-start | bytes 6291460
  545.4 5.4 copy-start.7
  545.4 5.4 copy-start.13
  550.8 11.2 %copy-start.40 = (bf16[512,2048]{1,0:T(8,128)(2,1)S(1)}, bf16[512,2048]{1,0:T(8,128)(2,1)}, u32[]{:S(2)}) copy-start(bf16[512,2048]{1,0:T(8,128)(2,1)} %get-tuple-element.61) | copy-start | bytes 6291460
  562.0 2.5 copy-start.14
  562.0 5.3 copy-start.17
  562.1 2.7 copy-start.36
  564.8 2.5 copy-start.35
  573.7 1.6 copy-start.16
  573.8 367.7 %reduce-scatter.4.cloned.1.call-start = ((), (), s32[]{:S(2)}) async-start(), calls=%async_computation.4 | async-start | bytes 9437184 | tf_op jit(solution)/shard_map/reduce_scatter | solution.py:1259
  575.3 1.2 copy-start.18
  580.7 1.1 copy-start.15
  586.7 1.3 copy-start.5
  660.6 1.6 copy-start.3
  660.6 1.8 copy-start.9
  660.7 315.2 %reduce-scatter.8.cloned.1.call-start = ((), (), s32[]{:S(2)}) async-start(), calls=%async_computation.6 | async-start | bytes 9437184 | tf_op jit(solution)/shard_map/reduce_scatter | solution.py:1270
  667.4 9.9 %copy-start.30 = (f32[1,2048]{1,0:T(1,128)S(1)}, f32[1,2048]{1,0:T(1,128)}, u32[]{:S(2)}) copy-start(f32[1,2048]{1,0:T(1,128)} %get-tuple-element.82) | copy-start | bytes 24580
  667.5 9.9 %copy-start.31 = (f32[1,2048]{1,0:T(1,128)S(1)}, f32[1,2048]{1,0:T(1,128)}, u32[]{:S(2)}) copy-start(f32[1,2048]{1,0:T(1,128)} %get-tuple-element.83) | copy-start | bytes 24580
  667.5 9.8 %copy-start.32 = (f32[1,2048]{1,0:T(1,128)S(1)}, f32[1,2048]{1,0:T(1,128)}, u32[]{:S(2)}) copy-start(f32[1,2048]{1,0:T(1,128)} %get-tuple-element.80) | copy-start | bytes 24580
  667.5 9.8 %copy-start.33 = (f32[1,2048]{1,0:T(1,128)S(1)}, f32[1,2048]{1,0:T(1,128)}, u32[]{:S(2)}) copy-start(f32[1,2048]{1,0:T(1,128)} %get-tuple-element.81) | copy-start | bytes 24580
  667.5 10.5 %copy-start.23 = (bf16[1024,2048]{1,0:T(8,128)(2,1)S(1)}, bf16[1024,2048]{1,0:T(8,128)(2,1)}, u32[]{:S(2)}) copy-start(bf16[1024,2048]{1,0:T(8,128)(2,1)} %get-tuple-element.75.refs_1_) | copy-start | bytes 12582916
  667.5 10.5 %copy-start.38 = (bf16[1,512,2048]{2,1,0:T(8,128)(2,1)S(1)}, bf16[1,512,2048]{2,1,0:T(8,128)(2,1)}, u32[]{:S(2)}) copy-start(bf16[1,512,2048]{2,1,0:T(8,128)(2,1)} %get-tuple-element.55) | copy-start | bytes 6291460
  676.0 1.3 copy-start.4
  680.3 19.2 %copy-start.11 = (bf16[1024,512]{1,0:T(8,128)(2,1)S(1)}, bf16[1024,512]{1,0:T(8,128)(2,1)}, u32[]{:S(2)}) copy-start(bf16[1024,512]{1,0:T(8,128)(2,1)} %copy-done.10) | copy-start | bytes 3145732
  699.6 3.8 copy-start.34
  699.6 12.8 %slice-start = ((s8[6291456]{0:T(1024)(128)(4,1)}), s8[4194304]{0:T(1024)(128)(4,1)S(1)}, s32[]{:S(2)}) async-start(s8[6291456]{0:T(1024)(128)(4,1)} %bitcast.105), calls=%async_computation.8 | async-start | bytes 8388608
  703.4 9.0 slice-start.1
  720.6 6.8 copy-start.22
  927.1 6.0 copy-start.26
  930.1 5.3 copy-start.24
  935.4 3.3 copy-start.29
  935.4 4.6 copy-start.27
  935.4 6.1 copy-start.21
  941.5 2.7 copy-start.25
  944.2 31.7 %copy-start.28 = (bf16[256,2048]{1,0:T(8,128)(2,1)S(1)}, bf16[256,2048]{1,0:T(8,128)(2,1)}, u32[]{:S(2)}) copy-start(bf16[256,2048]{1,0:T(8,128)(2,1)} %get-tuple-element.124) | copy-start | bytes 3145732
  944.2 32.6 %copy-start.1 = (s32[2,1024]{1,0:T(2,128)S(1)}, s32[2,1024]{1,0:T(2,128)}, u32[]{:S(2)}) copy-start(s32[2,1024]{1,0:T(2,128)} %param.28) | copy-start | bytes 24580
Sparse Core Ops, SparseCore 0:
  80.3 122.1 all-gather.1
  444.8 171.8 all-reduce.2
  620.1 87.1 reduce-scatter.5
  709.4 140.6 reduce-scatter.3
  852.8 122.9 reduce-scatter.7

commit v4 on v3

--- a/solution.py
+++ b/solution.py
@@ -1266,13 +1266,14 @@
     own_out = dot_t(e1, o1).astype(BF16)[None]
     p5 = planes_back(triple_back, w_self2)
     text_w_part = columns_dot(text, dproj)
-    p7 = rows_dot([dproj], w_text[None], 1024)
-    text_grad = lax.psum_scatter(p7, TENSOR, scatter_dimension=0, tiled=True)
+    p7, p8 = [rows_dot([dproj], part[None], 1024) for part in jnp.split(w_text, 2)]
+    text_right = lax.psum_scatter(p8, TENSOR, scatter_dimension=0, tiled=True)
     everyone = [(TENSOR, bit) for bit in bits_of(n_tensor)] + [(DP, bit) for bit in bits_of(n_dp)]
     late = jnp.concatenate([gain_one, shift_one, gain_two, shift_two])
     (
         (self_grad, self_out_grad),
         (unused, unused, image_grad, all_sums),
+        (text_left,),
         (cross_q_grad, cross_kv_grad, cross_out_grad),
         (text_w_grad,),
     ) = run_flows(
@@ -1291,11 +1292,13 @@
             everyone=everyone,
             clock=(6, 0, 8, 50),
         ),
+        stream_flow(terms=p7, rs=n_tensor, keep=False, clock=(7, 45, 11, 110)),
         grads_flow((cross_part,), n_dp, (1, 2, 0), half, summing=False, clock=(15, 12)),
         grads_flow((text_w_part.reshape(4, -1, width),), n_dp, (4,), clock=(10, 16)),
     )
     down_grad, up_grad = [value.astype(F32) for value in sums]
     self_grad, self_out_grad = self_grad.astype(F32), self_out_grad.astype(F32)
+    text_grad = jnp.concatenate([text_left, text_right], axis=1)
     cross_q_grad, cross_kv_grad = cross_q_grad[0].astype(F32), cross_kv_grad.astype(F32)
     cross_out_grad = cross_out_grad.astype(F32)
     text_w_grad = text_w_grad.reshape(-1, width).astype(F32)

time: 992 us -> 999 us (level)
  waiting for transfers between devices: 30 us -> 0.8 us
  Pallas kernels: 800 us -> 825 us
    reduce_scatter x1, waiting for transfers between devices: 29.2 us -> 0.01 us  [local(): text_right = lax.psum_scatter(p8, TENSOR, scatter_dimension=0, tiled=True)]
    pallas_call x6, Pallas kernels: 698 us -> 726 us  [run_flows(): pl.pallas_call(functools.partial(flows_kernel, flows), in_specs=[entry[1]...]
    pallas_call x4 -> x5, Pallas kernels: 26.4 us -> 24.9 us  [rows_dot(): pl.pallas_call(functools.partial(rows_dot_kernel, count), grid=(wide // t...]
  transfers between devices with their start and end apart: 5 -> 5, of which waited for: 1 -> 0; matrix products, arithmetic and copies ran while one was open for 10% -> 10% of each run, Pallas kernels for 59% -> 61%
where the time goes in v4:
time: 999 us; the launch traced here: 991 us
  Pallas kernels  825 us (83%)
  matrix products  92.3 us (9%)
  other arithmetic  38.6 us (4%)
  local copies, waits for them, and re-layouts  18.8 us (2%)
  between operations  14.5 us (1%)
    pallas_call x6, Pallas kernels, run_flows(): pl.pallas_call(functools.partial(flows_kernel, flows), in_specs=[entry[1]...  726 us
    dot_general x5, matrix products, dot_t(): lax.dot_general(left, right, (((0,), (0,)), ((), ())), preferred_element_...  37.2 us
    pallas_call x2, Pallas kernels, attend_back(): pl.pallas_call(functools.partial(attend_back_kernel, 256), grid=(heads,),...  30.1 us
    pallas_call x5, Pallas kernels, rows_dot(): pl.pallas_call(functools.partial(rows_dot_kernel, count), grid=(wide // t...  24.9 us
  transfers between devices with their start and end apart: 5, of which 0 were waited for; matrix products, arithmetic and copies ran while one was open for 10% of the time, Pallas kernels for 61%

profile of v4, /device:TPU:0, one launch (start us, length us, event | category | flops | bytes accessed | tf_op | source)
XLA Modules:
  0.0 990.7 jit_solution(10894499647214630147)
XLA Ops:
  7.2 1.5 fusion.41
  8.8 71.3 %start.1 = (bf16[3,2048,512]{2,1,0:T(8,128)(2,1)}, bf16[1,512,2048]{2,1,0:T(8,128)(2,1)}, bf16[1024,2048]{1,0:T(8,128)(2,1)}, bf16[256,2048]{1,0:T(8,128)(2,1)}, bf16[1024,256]{1,0:T(8,128)(2,1)}) custom-call(bf16[3,2048,256]{2,1,0:T(8,128)(2,1)} %refs_0_.2, bf16[1,256,2048]{2,1,0:T(8,128)(2,1)} %bitcast.103, bf16[256,2048]{1,0:T(8,128)(2,1)} %refs_2_.5, ...), custom_call_target="tpu_custom_call" | custom-call | bytes 198000000 | tf_op jit(solution)/shard_map/start/pallas_call | solution.py:386
  80.2 0.2 copy.41.qid_ref
  80.5 10.1 %convert_bitcast_fusion.2.q_ref.k_ref.v_ref = bf16[3,1024,512]{2,1,0:T(8,128)(2,1)S(1)} fusion(bf16[3,2048,512]{2,1,0:T(8,128)(2,1)} %get-tuple-element.54, bf16[1024,2048]{1,0:T(8,128)(2,1)} %get-tuple-element.55), kind=kOutput, calls=%fused_computation.12 | convolution fusion | flops 6444023808 | bytes 13631488 | tf_op jit(solution)/shard_map/td,cde->cte/dot_general | solution.py:215
  90.7 10.1 %attend.2 = bf16[1024,512]{1,0:T(8,128)(2,1)S(1)} custom-call(s32[1024,1]{1,0:T(8,128)S(1)} %copy.41.qid_ref, s32[1,1024]{1,0:T(1,128)S(1)} %constant_dynamic-slice_fusion.kid_ref, bf16[3,1024,512]{2,1,0:T(8,128)(2,1)S(1)} %convert_bitcast_fusion.2.q_ref.k_ref.v_ref, bf16[3,1024,512]{2,1,0:T(8,128)(2,1)S(1)} %convert_bitcast_fusion.2.q_ref.k_ref.v_ref, ...), custom_call_target="tpu_custom_call" | custom-call | flops 2147483648 | bytes 4194304 | tf_op jit(solution)/shard_map/attend/pallas_call | solution.py:88
  100.8 4.4 convolution_convert_fusion.2.refs_3_
  105.2 140.3 %self_sum.1 = (f32[256,2048]{1,0:T(8,128)}, bf16[1024,2048]{1,0:T(8,128)(2,1)}, bf16[2,2048,512]{2,1,0:T(8,128)(2,1)}, bf16[1,2048,512]{2,1,0:T(8,128)(2,1)}, bf...) custom-call(bf16[256,2048]{1,0:T(8,128)(2,1)} %refs_2_.5, f32[1,2048]{1,0:T(1,128)} %get-tuple-element.112.refs_1_, ...), custom_call_target="tpu_custom_call" | custom-call | bytes 330000000 | tf_op jit(solution)/shard_map/self_sum/pallas_call | solution.py:386
  245.6 5.3 fusion.31.k_ref.v_ref
  250.9 2.3 fusion.22.q_ref
  253.3 7.4 attend.3
  260.7 1.0 copy-done.11
  261.6 1.0 copy-done.9
  262.6 4.4 convolution_convert_fusion.1.refs_3_
  267.0 114.6 %cross_sum.1 = (f32[256,2048]{1,0:T(8,128)}, bf16[2048,2048]{1,0:T(8,128)(2,1)}, bf16[2048,1024]{1,0:T(8,128)(2,1)}) custom-call(f32[256,2048]{1,0:T(8,128)} %get-tuple-element.58.refs_0_, f32[1,2048]{1,0:T(1,128)} %get-tuple-element.113.refs_1_, f32[1,2048]{1,0:T(1,128)} %get-tuple-element.105.refs_2_, ...), custom_call_target="tpu_custom_call" | custom-call | bytes 330000000 | tf_op jit(solution)/shard_map/cross_sum/pallas_call | solution.py:386
  381.6 19.1 %hidden_step.1 = (bf16[2048,1024]{1,0:T(8,128)(2,1)S(1)}, bf16[2048,1024]{1,0:T(8,128)(2,1)}) custom-call(bf16[2048,2048]{1,0:T(8,128)(2,1)} %get-tuple-element.66.tokens_ref, bf16[2048,1024]{1,0:T(8,128)(2,1)} %weight_ref.1, bf16[2048,1024]{1,0:T(8,128)(2,1)} %get-tuple-element.67.back_ref), custom_call_target="tpu_custom_call" | custom-call | flops 8589934592 | bytes 25165824 | tf_op jit(solution)/shard_map/hidden_step/pallas_call | solution.py:254
  400.7 15.5 %convolution_convert_fusion.3.refs_2_ = bf16[2048,1024]{1,0:T(8,128)(2,1)} fusion(bf16[2048,2048]{1,0:T(8,128)(2,1)} %get-tuple-element.66.tokens_ref, bf16[2048,1024]{1,0:T(8,128)(2,1)} %get-tuple-element.68.refs_0_), kind=kOutput, calls=%fused_computation.10 | convolution fusion | flops 8592031744 | bytes 16777216 | tf_op jit(solution)/shard_map/dot_general | solution.py:148
  416.2 12.4 %rows_dot.5.refs_0_ = bf16[2048,2048]{1,0:T(8,128)(2,1)} custom-call(bf16[2048,1024]{1,0:T(8,128)(2,1)S(1)} %copy-done.19, bf16[1,2048,1024]{2,1,0:T(8,128)(2,1)} %bitcast.109), custom_call_target="tpu_custom_call" | custom-call | flops 8589934592 | bytes 16777216 | tf_op jit(solution)/shard_map/rows_dot/pallas_call | solution.py:169
  428.6 13.0 %convolution_convert_fusion.refs_1_ = bf16[1024,2048]{1,0:T(8,128)(2,1)} fusion(bf16[2048,1024]{1,0:T(8,128)(2,1)S(1)} %get-tuple-element.69.refs_4_, bf16[2048,2048]{1,0:T(8,128)(2,1)} %all-gather.2.cloned.1.call-done.refs_4_), kind=kOutput, calls=%fused_computation.7 | convolution fusion | flops 8592031744 | bytes 16777216 | tf_op jit(solution)/shard_map/dot_general | solution.py:148
  441.6 0.7 all-reduce.3.cloned.1.call-update
  442.3 0.4 reduce-scatter.6.cloned.1.call-start
  442.8 104.6 %up_sum.1 = (f32[1,2048]{1,0:T(1,128)}, f32[1,2048]{1,0:T(1,128)}, f32[256,2048]{1,0:T(8,128)}, bf16[1024,2048]{1,0:T(8,128)(2,1)}, bf16[2048,2048]{1,0:T(8,128)(2,1)}) custom-call(f32[256,2048]{1,0:T(8,128)} %get-tuple-element.65.refs_0_, f32[1,2048]{1,0:T(1,128)} %get-tuple-element.113.refs_1_, bf16[256,2048]{1,0:T(8,128)(2,1)} %refs_2_.4, ...), custom_call_target="tpu_custom_call" | custom-call | bytes 330000000 | tf_op jit(solution)/shard_map/up_sum/pallas_call | solution.py:386
  547.5 5.1 fusion.28.do_ref
  552.5 11.2 %attend_back.2 = (bf16[1024,512]{1,0:T(8,128)(2,1)S(1)}, bf16[512,512]{1,0:T(8,128)(2,1)S(1)}, bf16[512,512]{1,0:T(8,128)(2,1)S(1)}) custom-call(s32[1024,1]{1,0:T(8,128)S(1)} %copy.41.qid_ref, s32[1,512]{1,0:T(1,128)S(1)} %compare_select_fusion.kid_ref, bf16[1024,512]{1,0:T(8,128)(2,1)S(1)} %copy-done.12, bf16[2,512,512]{2,1,0:T(8,128)(2,1)S(1)} %fusion.31.k_ref.v_ref, ...), custom_call_target="tpu_custom_call" | custom-call | flops 2684354560 | bytes 5242880 | tf_op jit(solution)/shard_map/attend_back/pallas_call | solution.py:115
  563.8 2.4 convert_bitcast_fusion.1
  566.2 0.6 copy-done.36
  566.8 2.5 fusion.4
  569.3 2.4 fusion.3
  571.7 3.8 pad_maximum_fusion.refs_1_
  575.6 1.1 copy-done.18
  576.8 1.6 copy-done.16
  578.4 4.2 rows_dot.6.refs_0_
  582.6 1.1 copy-done.14
  583.6 4.8 rows_dot.7.refs_4_
  588.5 1.3 copy-done.5
  589.8 72.7 %query_sum.1 = (f32[1,2048]{1,0:T(1,128)}, f32[1,2048]{1,0:T(1,128)}, f32[256,2048]{1,0:T(8,128)}, bf16[1024,2048]{1,0:T(8,128)(2,1)}, bf16[1024,256]{1,0:T(8,128)(2,1)}) custom-call(f32[256,2048]{1,0:T(8,128)} %get-tuple-element.58.refs_0_, f32[1,2048]{1,0:T(1,128)} %get-tuple-element.112.refs_1_, f32[256,2048]{1,0:T(8,128)} %get-tuple-element.71.refs_2_, ...), custom_call_target="tpu_custom_call" | custom-call | bytes 198000000 | tf_op jit(solution)/shard_map/query_sum/pallas_call | solution.py:386
  662.6 0.4 reduce-scatter.8.cloned.1.call-start
  663.0 1.9 slice_bitcast_fusion
  665.0 1.8 rows_dot.9
  666.7 2.0 copy-done.3
  668.8 7.7 columns_dot.1
  676.5 1.3 copy-done.6
  677.8 0.7 copy-done.29
  678.5 0.6 pad_maximum_fusion.5.refs_6_
  679.2 1.7 rows_dot.8.refs_7_
  681.0 2.1 copy-done.4
  683.0 4.1 fusion.19.do_ref
  687.1 18.9 %attend_back.3 = (bf16[1024,512]{1,0:T(8,128)(2,1)S(1)}, bf16[1024,512]{1,0:T(8,128)(2,1)S(1)}, bf16[1024,512]{1,0:T(8,128)(2,1)S(1)}) custom-call(s32[1024,1]{1,0:T(8,128)S(1)} %copy.41.qid_ref, s32[1,1024]{1,0:T(1,128)S(1)} %constant_dynamic-slice_fusion.kid_ref, bf16[3,1024,512]{2,1,0:T(8,128)(2,1)} %copy-done.2, bf16[3,1024,512]{2,1,0:T(8,128)(2,1)} %copy-done.2, ...), custom_call_target="tpu_custom_call" | custom-call | flops 5368709120 | bytes 7340032 | tf_op jit(solution)/shard_map/attend_back/pallas_call | solution.py:115
  706.0 3.8 fusion.5.refs_1_
  709.7 8.9 convert_bitcast_fusion.refs_0_
  718.7 8.3 bitcast_convert_fusion.refs_5_
  727.0 6.9 convert_element_type.119
  733.8 4.5 convert_element_type.120
  738.3 221.9 %end.1 = (bf16[3,2048,256]{2,1,0:T(8,128)(2,1)}, bf16[256,2048]{1,0:T(8,128)(2,1)}, f32[1,2048]{1,0:T(1,128)}, f32[1,2048]{1,0:T(1,128)}, bf16[256,2048]{1,0:T(8...) custom-call(bf16[3,2048,512]{2,1,0:T(8,128)(2,1)} %convert_bitcast_f, ...), custom_call_target="tpu_custom_call" | custom-call | bytes 660000000 | tf_op jit(solution)/shard_map/end/pallas_call | solution.py:386
  960.2 5.3 convert_element_type.111
  965.5 2.3 convert_element_type.115
  967.8 1.6 convert_element_type.112
  969.4 1.6 convert_element_type.116
  971.0 0.6 pad_maximum_fusion.7
  971.6 0.6 pad_maximum_fusion.6
  972.3 1.5 bitcast_convert_fusion.2
  973.8 3.1 add_convert_fusion
  976.9 4.0 bitcast_convert_fusion.1
  980.9 2.1 pad_maximum_fusion.4
  983.0 1.0 copy.65
  (100 shorter events, 0.6 us)
Async XLA Ops:
  7.2 73.0 %copy-start = (s32[2,1024]{1,0:T(2,128)S(1)}, s32[2,1024]{1,0:T(2,128)}, u32[]{:S(2)}) copy-start(s32[2,1024]{1,0:T(2,128)} %param.28) | copy-start | bytes 24580
  7.2 259.8 %all-gather.2.cloned.1.call-start = ((), (), s32[]{:S(2)}) async-start(), calls=%async_computation.3 | async-start | bytes 9437184 | tf_op jit(solution)/shard_map/all_gather | solution.py:1168
  8.8 71.6 %copy-start.41 = (s32[8]{0:T(128)S(1)}, s32[8]{0:T(128)}, u32[]{:S(2)}) copy-start(s32[8]{0:T(128)} %param.29) | copy-start | bytes 100
  90.6 10.2 %copy-start.2 = (bf16[3,1024,512]{2,1,0:T(8,128)(2,1)}, bf16[3,1024,512]{2,1,0:T(8,128)(2,1)S(1)}, u32[]{:S(2)}) copy-start(bf16[3,1024,512]{2,1,0:T(8,128)(2,1)S(1)} %convert_bitcast_fusion.2.q_ref.k_ref.v_ref) | copy-start | bytes 9437188
  90.6 10.2 %copy-start.37 = (bf16[1,512,2048]{2,1,0:T(8,128)(2,1)S(1)}, bf16[1,512,2048]{2,1,0:T(8,128)(2,1)}, u32[]{:S(2)}) copy-start(bf16[1,512,2048]{2,1,0:T(8,128)(2,1)} %get-tuple-element.56) | copy-start | bytes 6291460
  245.6 5.3 copy-start.15
  245.6 5.3 copy-start.34
  253.3 9.3 copy-start.39
  260.7 1.0 copy-start.11
  261.6 1.0 copy-start.9
  400.7 27.9 %copy-start.8 = (bf16[2048,1024]{1,0:T(8,128)(2,1)}, bf16[2048,1024]{1,0:T(8,128)(2,1)S(1)}, u32[]{:S(2)}) copy-start(bf16[2048,1024]{1,0:T(8,128)(2,1)S(1)} %get-tuple-element.69.refs_4_) | copy-start | bytes 12582916
  400.7 15.5 %copy-start.19 = (bf16[2048,1024]{1,0:T(8,128)(2,1)S(1)}, bf16[2048,1024]{1,0:T(8,128)(2,1)}, u32[]{:S(2)}) copy-start(bf16[2048,1024]{1,0:T(8,128)(2,1)} %get-tuple-element.68.refs_0_) | copy-start | bytes 12582916
  441.6 285.4 %all-reduce.3.cloned.1.call-start = ((), (), s32[]{:S(2)}) async-start(), calls=%async_computation.7 | async-start | bytes 16777216 | tf_op jit(solution)/shard_map/psum | solution.py:1217
  442.3 296.0 %reduce-scatter.6.cloned.1.call-start = ((), (), s32[]{:S(2)}) async-start(), calls=%async_computation.5 | async-start | bytes 10485760 | tf_op jit(solution)/shard_map/reduce_scatter | solution.py:1240
  442.8 104.6 %copy-start.40 = (bf16[1,512,2048]{2,1,0:T(8,128)(2,1)S(1)}, bf16[1,512,2048]{2,1,0:T(8,128)(2,1)}, u32[]{:S(2)}) copy-start(bf16[1,512,2048]{2,1,0:T(8,128)(2,1)} %get-tuple-element.63) | copy-start | bytes 6291460
  547.4 5.1 copy-start.12
  552.5 11.2 %copy-start.38 = (bf16[512,2048]{1,0:T(8,128)(2,1)S(1)}, bf16[512,2048]{1,0:T(8,128)(2,1)}, u32[]{:S(2)}) copy-start(bf16[512,2048]{1,0:T(8,128)(2,1)} %get-tuple-element.62) | copy-start | bytes 6291460
  563.7 2.5 copy-start.13
  563.7 5.5 copy-start.17
  563.8 2.4 copy-start.10
  563.8 3.0 copy-start.36
  566.8 2.5 copy-start.35
  575.6 1.2 copy-start.18
  575.6 398.2 %reduce-scatter.4.cloned.1.call-start = ((), (), s32[]{:S(2)}) async-start(), calls=%async_computation.4 | async-start | bytes 9437184 | tf_op jit(solution)/shard_map/reduce_scatter | solution.py:1259
  576.8 1.6 copy-start.16
  582.6 1.1 copy-start.14
  588.5 1.3 copy-start.5
  662.5 2.4 copy-start.7
  662.6 318.4 %reduce-scatter.8.cloned.1.call-start = ((), (), s32[]{:S(2)}) async-start(), calls=%async_computation.6 | async-start | bytes 4718592 | tf_op jit(solution)/shard_map/reduce_scatter | solution.py:1270
  666.7 2.0 copy-start.3
  676.5 1.3 copy-start.6
  677.8 0.7 copy-start.29
  677.8 0.7 copy-start.30
  677.8 0.7 copy-start.31
  677.8 0.7 copy-start.32
  677.8 5.2 copy-start.21
  680.9 2.1 copy-start.4
  706.0 3.8 copy-start.33
  706.0 12.7 %slice-start = ((s8[6291456]{0:T(1024)(128)(4,1)}), s8[4194304]{0:T(1024)(128)(4,1)S(1)}, s32[]{:S(2)}) async-start(s8[6291456]{0:T(1024)(128)(4,1)} %bitcast.107), calls=%async_computation.8 | async-start | bytes 8388608
  709.7 8.9 slice-start.1
  727.0 6.9 copy-start.20
  960.2 5.3 copy-start.22
  965.5 2.4 copy-start.25
  965.5 3.9 copy-start.24
  967.8 3.1 copy-start.28
  967.8 4.4 copy-start.23
  976.9 4.1 copy-start.27
  976.9 7.1 copy-start.1
  976.9 6.2 copy-start.26
Sparse Core Ops, SparseCore 0:
  80.3 122.8 all-gather.1
  446.8 171.8 all-reduce.2
  622.0 87.1 reduce-scatter.5
  711.3 151.6 reduce-scatter.3
  865.1 85.5 reduce-scatter.7
